TPU v7x, 128 devices: a whole 4x4x4 slice. The times are simulated.
128 devices in a mesh: wide: 16 (over z, y), narrow: 8 (over x, core).
Axes of the slice: x: 4, y: 4, z: 4, core: 2. Of those that a mesh axis runs over, the one named last changes fastest.
Arguments:
- tokens: bfloat16 [22528, 1024], P(('wide', 'narrow')), may hold values from -6 to 6
- layer_cotangent: bfloat16 [22528, 1024], P(('wide', 'narrow')), may hold values from -6 to 6
- attn_gain: float32 [1024], replicated, may hold values from 0.25 to 1.75
- qkv_weight: float32 [3, 1024, 1024], P(None, None, 'narrow'), may hold values from -0.1875 to 0.1875
- out_weight: float32 [1024, 1024], P('narrow'), may hold values from -2.5 to 2.5
- rel_bias: float32 [16, 32], P('narrow'), may hold values from -4 to 4
- moe_gain: float32 [1024], replicated, may hold values from 0.25 to 1.75
- router_weight: float32 [1024, 32], replicated, may hold values from -0.125 to 0.125
- expert_in: float32 [32, 2, 1024, 2816], P('wide', None, None, 'narrow'), may hold values from -0.1875 to 0.1875
- expert_out: float32 [32, 2816, 1024], P('wide', 'narrow'), may hold values from -0.15625 to 0.15625
- routes: int32 [22528, 2], P(('wide', 'narrow')), may hold values from 0 to 31, all different within a row; in each aligned block of 176 rows (0 to 175, 176 to 351, ...) at most 26 rows name the same one
- buckets: int32 [2815], replicated, may hold values from 0 to 31, as said below
Outputs:
- layer_out: bfloat16 [22528, 1024], P(('wide', 'narrow'))
- input_grad: float32 [22528, 1024], P(('wide', 'narrow'))
- attn_gain_grad: float32 [1024], replicated
- qkv_weight_grad: float32 [3, 1024, 1024], P(None, None, 'narrow')
- out_weight_grad: float32 [1024, 1024], P('narrow')
- rel_bias_grad: float32 [16, 32], P('narrow')
- moe_gain_grad: float32 [1024], replicated
- router_grad: float32 [1024, 32], replicated
- expert_in_grad: float32 [32, 2, 1024, 2816], P('wide', None, None, 'narrow')
- expert_out_grad: float32 [32, 2816, 1024], P('wide', 'narrow')
Inputs may be any that keep to these rules, and one draw needn't show every extreme that they name: `routes`: each row names 2 different experts; within each aligned block of 176 rows no expert is named more than 2 * 13 times. Entry 1407 + j - i is the bucket of key position j for query position i of the same sequence; entry 1407 is 0; keys at or after the query use buckets below 16, keys before it the others.
All inputs are finite; a program needn't handle non-finite values.
Results may differ from a plain program's by a relative error of at most 0.02.
Values may be sent and summed in bfloat16 or wider, within the bound.
No kernel may reach another device: no remote copies, remote signals or barrier semaphores. Data moves between devices by JAX's collectives and lax.ppermute only.
A program may use at most 320 MiB of HBM per device.

v0:
```python
import functools
import math

import jax
import jax.numpy as jnp
from jax import lax
from jax.experimental import pallas as pl
from jax.experimental.pallas import tpu as pltpu
from jax.sharding import PartitionSpec as P

HEAD_DIM = 64
EXPERTS = 32
BUCKETS = 32
TOP = 2
LEN = 1408
WIDTH = 1024
TOK = 176
CAP = 13
SLOTS = 16
EPSILON = 1e-06
BLOCK = 128
SPAN = 2816
LOG2E = math.log2(math.e)
SCORE = LOG2E / 8
HIGHEST = lax.Precision.HIGHEST
F32 = jnp.float32
BF16 = jnp.bfloat16
NT = (((1,), (1,)), ((), ()))
TN = (((0,), (0,)), ((), ()))
VMEM = pl.BlockSpec(memory_space=pltpu.VMEM)
SMEM = pl.BlockSpec(memory_space=pltpu.SMEM)
HBM = pl.BlockSpec(memory_space=pl.ANY)
HIDDEN = 352
PADDED = 384
FULL = 2 * PADDED
ROWS = 416
HALF = 208
TILED = 432


def shape(dims, dtype):
    return jax.ShapeDtypeStruct(dims, dtype)


COSTS = {
    "dispatch": 50,
    "slots": 50,
    "collect": 50,
    "down_grad": 50,
    "halves": 50,
    "attend_forward": 4,
    "attend_backward": 50,
    "assemble_down": 50,
    "expert": 50,
    "pair_grad": 3,
    "share": 50,
}


MEBIBYTES = {
    "attend_forward": 30,
    "attend_backward": 56,
    "dispatch": 56,
    "halves": 56,
    "expert": 40,
    "middle_grad": 56,
    "down_grad": 56,
    "assemble_pair": 56,
    "assemble_down": 56,
}


def call(kernel, name, out_shape, ins, scratch=(), smem=0, hbm=0):
    outs = tuple(out_shape)
    return pl.pallas_call(
        kernel,
        out_shape=outs,
        in_specs=[SMEM] * smem + [HBM] * hbm + [VMEM] * (len(ins) - smem - hbm),
        out_specs=tuple([VMEM] * len(outs)),
        scratch_shapes=list(scratch),
        compiler_params=pltpu.CompilerParams(vmem_limit_bytes=MEBIBYTES.get(name, 24) << 20),
        cost_estimate=pl.CostEstimate(
            flops=int(COSTS.get(name, 0.1) * 1.15e9), bytes_accessed=0, transcendentals=0
        ),
        name=name,
    )(*ins)


def dot(a, b, dims=None, precision=None):
    if dims is None:
        dims = (((1,), (0,)), ((), ()))
    return lax.dot_general(a, b, dims, precision=precision, preferred_element_type=F32)


def block_of(i):
    return pl.ds(pl.multiple_of(i * BLOCK, BLOCK), BLOCK)


def offset_row(buckets, bias_ref, head):
    total = jnp.zeros(buckets.shape, F32)
    for bucket in range(BUCKETS):
        total = jnp.where(buckets == bucket, bias_ref[head, bucket], total)
    return total


def skew(row):
    return pltpu.roll(
        jnp.broadcast_to(row, (BLOCK, SPAN)), SPAN - (BLOCK - 1), 1, stride=1, stride_axis=0
    )


def spread_terms(value):
    lane = iota(value.shape, 1) % HEAD_DIM
    high = value.astype(BF16).astype(F32)
    rest = value - high
    middle = rest.astype(BF16).astype(F32)
    terms = jnp.where(lane == 0, high, jnp.where(lane == 1, middle, rest - middle))
    return jnp.where(lane < 3, terms, 0.0).astype(BF16)


def by_head(value, low):
    zero = jnp.zeros_like(value)
    return jnp.concatenate([jnp.where(low, value, zero), jnp.where(low, zero, value)], axis=0)


def attend_forward_kernel(place_ref, bias_ref, *refs):
    shards = refs[:8]
    (gain_ref, w_ref, buckets_ref, h_ref, qkv_ref, o_ref, proj_ref,
     band, value_parts) = refs[8:]
    count = LEN // BLOCK
    for head in range(2):
        band[head * BLOCK : (head + 1) * BLOCK, :] = skew(
            offset_row(buckets_ref[...], bias_ref, head) * LOG2E
        )
    weights = jnp.concatenate([w_ref[c].astype(BF16) for c in range(3)], axis=1)
    value_parts[:, 128:] = jnp.ones((LEN, 128), BF16)
    for index, shard in enumerate(shards):
        rows = pl.ds(pl.multiple_of(place_ref[index] * TOK, TOK), TOK)
        x = shard[...].astype(F32)
        scale = lax.rsqrt(jnp.mean(x * x, axis=-1, keepdims=True) + EPSILON)
        normed = (x * scale * gain_ref[...]).astype(BF16)
        h_ref[rows, :] = normed
        projected = dot(normed, weights).astype(BF16)
        qkv_ref[rows, :128] = (projected[:, :128].astype(F32) * SCORE).astype(BF16)
        qkv_ref[rows, 256:] = projected[:, 128:]
        value_parts[rows, :128] = projected[:, 256:]
    for c in range(3):
        proj_ref[c * 128 : (c + 1) * 128, :] = w_ref[c].T.astype(BF16)
    low = iota((BLOCK, 128), 1) < HEAD_DIM

    def attend(i, carry):
        rows = block_of(i)
        window = pl.ds(pl.multiple_of((count - 1 - i) * BLOCK, BLOCK), LEN)
        query = by_head(qkv_ref[rows, :128], low)
        scores = dot(query, qkv_ref[:, 256:384], NT) + band[:, window]
        peaks = jnp.max(scores, axis=-1, keepdims=True)
        weights = jnp.exp2(scores - peaks).astype(BF16)
        both = dot(weights, value_parts[...])
        parts = [both[:BLOCK], both[BLOCK:]]
        peaks = [peaks[:BLOCK], peaks[BLOCK:]]
        top = jnp.where(low, parts[0][:, :128], parts[1][:, :128])
        totals = jnp.where(low, parts[0][:, 128:], parts[1][:, 128:])
        o_ref[rows, :] = (top / totals).astype(BF16)
        logs = jnp.where(low, peaks[0], peaks[1]) + jnp.log2(totals)
        qkv_ref[rows, 128:256] = spread_terms(-logs)
        return carry

    lax.fori_loop(0, count, attend, 0, unroll=True)


def attend_forward(places, bias, shards, gain, weights, buckets):
    head = (LEN, 128)
    return call(
        attend_forward_kernel,
        "attend_forward",
        [
            shape((LEN, WIDTH), BF16),
            shape((LEN, 512), BF16),
            shape(head, BF16),
            shape((384, WIDTH), BF16),
        ],
        [places, bias, *shards, gain, weights, buckets],
        [pltpu.VMEM((2 * BLOCK, SPAN), F32), pltpu.VMEM((LEN, 256), BF16)],
        smem=2,
    )


def attend_backward_kernel(
    order_ref, bias_ref, normed_hbm, qkv_ref, o_ref, do_ref, buckets_ref, proj_ref, gain_ref,
    bias_grad_ref, weight_ref, gain_grad_ref, sent_ref, kept_ref,
    band, band_grad, query_grad, outs, low_grads, normed, sem,
):
    fetch = pltpu.make_async_copy(normed_hbm, normed, sem)
    fetch.start()
    count = LEN // BLOCK
    for head in range(2):
        band[head * BLOCK : (head + 1) * BLOCK, :] = skew(
            offset_row(buckets_ref[...], bias_ref, head) * LOG2E
        )
    band_grad[...] = jnp.zeros_like(band_grad)
    query_grad[...] = jnp.zeros_like(query_grad)
    low = iota((BLOCK, 128), 1) < HEAD_DIM

    def prepare(i, carry):
        rows = block_of(i)
        grads = do_ref[rows, :]
        products = grads.astype(F32) * o_ref[rows, :].astype(F32)
        one = jnp.sum(jnp.where(low, products, 0.0), axis=1, keepdims=True)
        two = jnp.sum(jnp.where(low, 0.0, products), axis=1, keepdims=True)
        low_grads[rows, :128] = grads
        low_grads[rows, 128:] = spread_terms(-jnp.where(low, one, two))
        return carry

    lax.fori_loop(0, count, prepare, 0)
    lane = iota((2 * BLOCK, 128), 1) - HEAD_DIM * (iota((2 * BLOCK, 128), 0) // BLOCK)
    terms = ((lane >= 0) & (lane < 3)).astype(F32).astype(BF16)

    def step(j, carry):
        rows = block_of(j)
        window = pl.ds(pl.multiple_of((count - 1 - j) * BLOCK, BLOCK), LEN)
        keys = by_head(qkv_ref[rows, 256:384], low)
        values = by_head(qkv_ref[rows, 384:], low)
        scores = dot(jnp.concatenate([keys, terms], axis=1), qkv_ref[:, :256], NT)
        probs = jnp.exp2(scores + band[:, window])
        score_grads = probs * dot(jnp.concatenate([values, terms], axis=1), low_grads[...], NT)
        band_grad[:, window] += score_grads
        score_low = score_grads.astype(BF16)
        value_grad = dot(probs.astype(BF16), low_grads[:, :128])
        key_grad = dot(score_low, qkv_ref[:, :128])
        query_grad[...] += dot(keys, score_low, TN)
        key_grad = jnp.where(low, key_grad[:BLOCK], key_grad[BLOCK:])
        outs[rows, 128:256] = (key_grad * (1.0 / LOG2E)).astype(BF16)
        outs[rows, 256:384] = jnp.where(low, value_grad[:BLOCK], value_grad[BLOCK:]).astype(BF16)
        return carry

    lax.fori_loop(0, count, step, 0, unroll=True)

    def turn(j, carry):
        rows = block_of(j)
        outs[rows, 0:128] = (query_grad[:, rows].T * 0.125).astype(BF16)
        return carry

    lax.fori_loop(0, count, turn, 0)
    for step, ref in enumerate([kept_ref] * 4 + [sent_ref] * 4):
        at = pl.ds(pl.multiple_of(order_ref[step] * TOK, TOK), TOK)
        ref[step % 4] = dot(outs[at, :], proj_ref[...]).astype(BF16)
    fetch.wait()
    total = dot(outs[...], normed[...], TN)
    weight_ref[:384, :] = total.astype(BF16)
    gain_grad_ref[...] = jnp.sum(total * proj_ref[...].astype(F32), axis=0, keepdims=True) / gain_ref[...]
    hot = buckets_ref[...] == iota((BUCKETS, SPAN), 0)
    for head in range(2):
        total = jnp.zeros((8, SPAN), F32)
        for group in range(BLOCK // 8):
            total = total + pltpu.roll(
                band_grad[head * BLOCK + group * 8 : head * BLOCK + (group + 1) * 8, :],
                (BLOCK - 1 - 8 * group) % SPAN,
                1,
            )
        row = jnp.zeros((1, SPAN), F32)
        for part in range(8):
            row = row + pltpu.roll(total, (SPAN - part) % SPAN, 1)[part : part + 1]
        by_bucket = jnp.sum(jnp.where(hot, row, 0.0), axis=1, keepdims=True)
        bias_grad_ref[head : head + 1, :] = jnp.broadcast_to(by_bucket, (BUCKETS, 128)).T[0:1]


def attend_backward(order, bias, normed, qkv, o, head_grads, buckets, proj, gain):
    return call(
        attend_backward_kernel,
        "attend_backward",
        [
            shape((2, BUCKETS), F32),
            shape((512, WIDTH), BF16),
            shape((1, WIDTH), F32),
            shape((4, TOK, WIDTH), BF16),
            shape((4, TOK, WIDTH), BF16),
        ],
        [order, bias, normed, qkv, o, head_grads, buckets, proj, gain],
        [
            pltpu.VMEM((2 * BLOCK, SPAN), F32),
            pltpu.VMEM((2 * BLOCK, SPAN), F32),
            pltpu.VMEM((128, LEN), F32),
            pltpu.VMEM((LEN, 384), BF16),
            pltpu.VMEM((LEN, 256), BF16),
            pltpu.VMEM((LEN, WIDTH), BF16),
            pltpu.SemaphoreType.DMA(()),
        ],
        smem=2,
        hbm=1,
    )


def iota(dims, axis):
    return lax.broadcasted_iota(jnp.int32, dims, axis)


def spread_kernel(turned_ref, routes_ref, cot_ref, picks_ref, place_ref, grads_ref):
    down = iota((EXPERTS, TOK), 0)
    before = (iota((TOK, TOK), 0) < iota((TOK, TOK), 1)).astype(BF16)
    named = [turned_ref[c : c + 1, :] == down for c in range(TOP)]
    earlier = [dot(n.astype(BF16), before) for n in named]
    earlier[1] = earlier[1] + jnp.sum(named[0].astype(F32), axis=1, keepdims=True)
    cells = iota((EXPERTS * SLOTS, TOK), 0)
    picks = jnp.zeros((EXPERTS * SLOTS, TOK), F32)
    for c in range(TOP):
        place = jnp.sum(jnp.where(named[c], earlier[c], 0.0), axis=0, keepdims=True).astype(jnp.int32)
        slot = jnp.where(place < CAP, turned_ref[c : c + 1, :] * SLOTS + place, -1)
        picks = picks + (cells == slot).astype(F32)
    picks = picks.astype(BF16)
    picks_ref[...] = picks
    grads_ref[...] = dot(picks, cot_ref[...]).astype(BF16)
    across = iota((TOK, EXPERTS), 1)
    after = (iota((TOK, TOK), 1) < iota((TOK, TOK), 0)).astype(BF16)
    named = [routes_ref[:, c : c + 1] == across for c in range(TOP)]
    earlier = [dot(after, n.astype(BF16)) for n in named]
    earlier[1] = earlier[1] + jnp.sum(named[0].astype(F32), axis=0, keepdims=True)
    for c in range(TOP):
        place = jnp.sum(jnp.where(named[c], earlier[c], 0.0), axis=1, keepdims=True)
        place_ref[:, c : c + 1] = place.astype(jnp.int32)


def split_low(value):
    high = value.astype(BF16)
    return high, (value - high.astype(F32)).astype(BF16)


def embed(values):
    rows = iota((EXPERTS * SLOTS, EXPERTS), 0)
    first = iota((EXPERTS * SLOTS, EXPERTS), 1) * SLOTS + CAP
    high, low = split_low(values)
    return dot((rows == first).astype(BF16), high) + dot((rows == first + 1).astype(BF16), low)


def dispatch_kernel(order_ref, heads_ref, *refs):
    wouts = refs[:8]
    (tok_ref, gain_ref, router_ref, routes_ref, place_ref, picks_ref,
     middle_ref, gates_ref, rows_ref, all_ref) = refs[8:]
    for index, part in enumerate(wouts):
        at = pl.ds(pl.multiple_of(order_ref[index] * 128, 128), 128)
        all_ref[at, :] = part[...]
    heads = jnp.concatenate([heads_ref[n] for n in range(8)], axis=1)
    middle = tok_ref[...].astype(F32) + dot(heads, all_ref[...])
    middle_ref[...] = middle
    scale = lax.rsqrt(jnp.mean(middle * middle, axis=-1, keepdims=True) + EPSILON)
    normed = middle * scale * gain_ref[...]
    rows_ref[...] = dot(picks_ref[...], normed.astype(BF16)).astype(BF16)
    logits = dot(normed, router_ref[...], NT, HIGHEST)
    across = iota((TOK, EXPERTS), 1)
    named = [routes_ref[:, c : c + 1] == across for c in range(TOP)]
    picked = [jnp.sum(jnp.where(n, logits, 0.0), axis=1, keepdims=True) for n in named]
    peak = jnp.maximum(picked[0], picked[1])
    powers = [jnp.exp(p - peak) for p in picked]
    total = powers[0] + powers[1]
    table = jnp.zeros((EXPERTS, 128), F32)
    for c in range(TOP):
        gate = powers[c] / total
        gates_ref[:, c : c + 1] = gate
        spot = (iota((TOK, 128), 1) == place_ref[:, c : c + 1]) & (place_ref[:, c : c + 1] < CAP)
        expert = named[c].astype(F32).astype(BF16)
        high, low = split_low(gate)
        for term in (high, low):
            table = table + dot(expert, jnp.where(spot, term.astype(F32), 0.0).astype(BF16), TN)
    rows_ref[:, :128] = (rows_ref[:, :128].astype(F32) + embed(table)).astype(BF16)


def slots_kernel(routes_ref, place_ref, picks_ref):
    cells = iota((TOK, EXPERTS * SLOTS), 1)
    for c in range(TOP):
        place = place_ref[:, c : c + 1]
        slot = jnp.where(place < CAP, routes_ref[:, c : c + 1] * SLOTS + place, -1)
        picks_ref[c] = (cells == slot).astype(F32).astype(BF16)


def middle_grad_kernel(
    rows_ref, gates_ref, middle_ref, cot_ref, routes_ref, place_ref, picks_ref, gain_ref, router_ref, wout_ref,
    middle_grad_ref, low_ref, heads_ref, gain_grad_ref, logit_ref,
):
    spots = iota((EXPERTS, EXPERTS * SLOTS), 1)
    first = iota((EXPERTS, EXPERTS * SLOTS), 0) * SLOTS + CAP
    packed = rows_ref[:, :128]
    table = [dot((spots == first + step).astype(BF16), packed).astype(BF16) for step in range(2)]
    across = iota((TOK, EXPERTS), 1)
    named = [routes_ref[:, c : c + 1] == across for c in range(TOP)]
    gates = [gates_ref[:, c : c + 1] for c in range(TOP)]
    gate_grads = []
    for c in range(TOP):
        expert = named[c].astype(F32).astype(BF16)
        lines = dot(expert, table[0]) + dot(expert, table[1])
        place = place_ref[:, c : c + 1]
        spot = (iota((TOK, 128), 1) == place) & (place < CAP)
        gate_grads.append(jnp.sum(jnp.where(spot, lines, 0.0), axis=1, keepdims=True))
    mean = gates[0] * gate_grads[0] + gates[1] * gate_grads[1]
    logit_grads = sum(
        jnp.where(n, g * (d - mean), 0.0) for n, g, d in zip(named, gates, gate_grads)
    )
    logit_ref[...] = logit_grads
    normed_grad = dot(logit_grads, router_ref[...], precision=HIGHEST)
    for c, gate in enumerate(gates):
        normed_grad = normed_grad + gate * dot(picks_ref[c], rows_ref[...])
    middle = middle_ref[...]
    scale = lax.rsqrt(jnp.mean(middle * middle, axis=-1, keepdims=True) + EPSILON)
    unit = middle * scale
    gain_grad_ref[...] = jnp.sum(normed_grad * unit, axis=0, keepdims=True)
    weighted = normed_grad * gain_ref[...]
    middle_grad = cot_ref[...].astype(F32) + scale * (
        weighted - unit * jnp.mean(weighted * unit, axis=-1, keepdims=True)
    )
    middle_grad_ref[...] = middle_grad
    low = middle_grad.astype(BF16)
    low_ref[...] = low
    for n in range(8):
        heads_ref[n] = dot(low, wout_ref[n * 128 : (n + 1) * 128, :], NT).astype(BF16)


def combine_kernel(rows_ref, middle_ref, gates_ref, picks_ref, layer_ref):
    layer = middle_ref[...]
    mixed = jnp.zeros_like(layer)
    for c in range(TOP):
        mixed = mixed + gates_ref[:, c : c + 1] * dot(picks_ref[c], rows_ref[...])
    layer_ref[...] = (layer + mixed).astype(BF16)


CUBIC = 0.044715
ROOT = math.sqrt(2.0 / math.pi)


def unpack_kernel(gated, blocks_ref, rows_ref):
    at = iota((ROWS, EXPERTS * SLOTS), 0)
    pick = (at // CAP) * SLOTS + at % CAP == iota((ROWS, EXPERTS * SLOTS), 1)
    rows_ref[:ROWS, :] = dot(pick.astype(F32).astype(BF16), blocks_ref[...]).astype(BF16)
    if gated:
        spots = iota((EXPERTS, EXPERTS * SLOTS), 1)
        first = iota((EXPERTS, EXPERTS * SLOTS), 0) * SLOTS + CAP
        lane = iota((128, ROWS), 1) % CAP == iota((128, ROWS), 0)
        mine = iota((EXPERTS, ROWS), 1) // CAP == iota((EXPERTS, ROWS), 0)
        rows_ref[ROWS:, :] = jnp.zeros((TILED - ROWS, WIDTH), BF16)
        terms = []
        for step in range(2):
            table = dot((spots == first + step).astype(BF16), blocks_ref[:, :128]).astype(BF16)
            spread = dot(table, lane.astype(F32).astype(BF16))
            terms.append(jnp.sum(jnp.where(mine, spread, 0.0), axis=0, keepdims=True))
        rows_ref[ROWS:, :ROWS] = stack_terms(*terms)


def stack_terms(high, low):
    step = iota((TILED - ROWS, ROWS), 0)
    return jnp.where(step == 0, high, jnp.where(step == 1, low, 0.0)).astype(BF16)


def unpack(blocks, gated):
    return call(
        functools.partial(unpack_kernel, gated),
        "unpack",
        [shape((TILED if gated else ROWS, WIDTH), BF16)],
        [blocks.reshape(EXPERTS * SLOTS, WIDTH)],
    )[0]


def expert_kernel(counts, *refs):
    groups = []
    for count in counts:
        groups.append(refs[: count + 1])
        refs = refs[count + 1 :]
    pair_ref, pair_new_ref, down_ref, down_new_ref = refs[:4]
    refs = refs[4:]
    for *rows_refs, grads_ref in groups:
        mid_ref, inner_ref, out_top_ref, out_end_ref, back_top_ref, back_end_ref = refs[:6]
        refs = refs[6:]
        if len(rows_refs) == 1:
            rows = rows_refs[0][:ROWS, :]
        else:
            rows = jnp.concatenate([rows_refs[0][...], rows_refs[1][:HALF, :]], axis=0)
        one = dot(rows, pair_ref[...], NT)
        two = dot(rows, pair_new_ref[...], NT)
        gate = jnp.concatenate([one[:, :PADDED], two[:, :PADDED]], axis=1)
        up = jnp.concatenate([one[:, PADDED:], two[:, PADDED:]], axis=1)
        down = jnp.concatenate([down_ref[...], down_new_ref[...]], axis=0)
        mid_grad = dot(grads_ref[...], down, NT)
        square = gate * gate
        turned = jnp.tanh(ROOT * gate * (1.0 + CUBIC * square))
        half = 0.5 * (1.0 + turned)
        curved = gate * half
        slope = half + 0.5 * gate * (1.0 - turned * turned) * (ROOT * (1.0 + 3.0 * CUBIC * square))
        mid = (curved * up).astype(BF16)
        mid_ref[...] = mid
        gate_grad = (mid_grad * (up * slope)).astype(BF16)
        up_grad = (mid_grad * curved).astype(BF16)
        for part in range(2):
            cut = slice(part * PADDED, (part + 1) * PADDED)
            inner_ref[:, 2 * part * PADDED : (2 * part + 1) * PADDED] = gate_grad[:, cut]
            inner_ref[:, (2 * part + 1) * PADDED : (2 * part + 2) * PADDED] = up_grad[:, cut]
        product = (mid.astype(F32) * mid_grad).astype(BF16)
        line = dot(jnp.ones((8, FULL), BF16), product, NT)[0:1]
        high, low = split_low(line)
        back_end_ref[HALF:, :] = jnp.zeros((TILED - ROWS, WIDTH), BF16)
        back_end_ref[HALF:, :ROWS] = stack_terms(high.astype(F32), low.astype(F32))
        pair = jnp.concatenate([pair_ref[...], pair_new_ref[...]], axis=0)
        back = dot(inner_ref[...], pair).astype(BF16)
        back_top_ref[...] = back[:HALF]
        back_end_ref[:HALF, :] = back[HALF:]
        out = dot(mid_ref[...], down).astype(BF16)
        out_top_ref[...] = out[:HALF]
        out_end_ref[...] = out[HALF:]


def run_expert(chunks, weights):
    results = call(
        functools.partial(expert_kernel, [len(rows) for rows, _ in chunks]),
        "expert",
        [
            shape((ROWS, FULL), BF16),
            shape((ROWS, 2 * FULL), BF16),
            shape((HALF, WIDTH), BF16),
            shape((HALF, WIDTH), BF16),
            shape((HALF, WIDTH), BF16),
            shape((TILED - HALF, WIDTH), BF16),
        ]
        * len(chunks),
        [a for rows, grads in chunks for a in (*rows, grads)] + weights,
    )
    return [list(results[6 * i : 6 * i + 6]) for i in range(len(chunks))]


def join_kernel(
    own_top, own_end, near_top, near_end, left_top, far_top, right_end, far_end,
    left_out, right_out, part_top, part_end,
):
    left_out[...] = (left_top[...].astype(F32) + far_top[...].astype(F32)).astype(BF16)
    right_out[...] = (right_end[...].astype(F32) + far_end[...].astype(F32)).astype(BF16)
    part_top[...] = own_top[...].astype(F32) + near_top[...].astype(F32)
    part_end[...] = own_end[...].astype(F32) + near_end[...].astype(F32)


def join(*pieces):
    return call(
        join_kernel,
        "join",
        [shape(p.shape, t) for t, p in ((BF16, pieces[0]), (BF16, pieces[1]), (F32, pieces[0]), (F32, pieces[1]))],
        pieces,
    )


def spread_slots(rows, out_ref):
    at = iota((EXPERTS * SLOTS, ROWS), 1)
    pick = iota((EXPERTS * SLOTS, ROWS), 0) == (at // CAP) * SLOTS + at % CAP
    out_ref[...] = dot(pick.astype(F32).astype(BF16), rows.astype(BF16)).astype(BF16)


def collect_kernel(part_top, part_end, got_top, got_end, out_ref):
    end = part_end[...] + got_end[...].astype(F32)
    rows = jnp.concatenate([part_top[...] + got_top[...].astype(F32), end[:HALF]], axis=0)
    spread_slots(rows, out_ref)
    line = jnp.sum(end[HALF:, :ROWS], axis=0, keepdims=True)
    mine = iota((EXPERTS, ROWS), 1) // CAP == iota((EXPERTS, ROWS), 0)
    spot = (iota((ROWS, 128), 0) % CAP == iota((ROWS, 128), 1)).astype(F32).astype(BF16)
    table = jnp.zeros((EXPERTS, 128), F32)
    for term in split_low(line):
        table = table + dot(jnp.where(mine, term.astype(F32), 0.0).astype(BF16), spot)
    out_ref[:, :128] = (out_ref[:, :128].astype(F32) + embed(table)).astype(BF16)


def collect_out_kernel(part_top, part_end, got_top, got_end, out_ref):
    top = part_top[...] + got_top[...].astype(F32)
    end = part_end[...] + got_end[...].astype(F32)
    spread_slots(jnp.concatenate([top, end], axis=0), out_ref)


def put_weight_grads(lefts, scaled, targets):
    width = 256
    for base in range(0, len(targets) * PADDED, width):
        total = jnp.zeros((width, WIDTH), F32)
        for chunk in range(4):
            at = slice(chunk * ROWS, (chunk + 1) * ROWS)
            total = total + dot(lefts[chunk][:, base : base + width], scaled[at, :], TN)
        for index, target in enumerate(targets):
            start = max(base, index * PADDED)
            stop = min(base + width, index * PADDED + HIDDEN)
            if start < stop:
                part = total[start - base : stop - base]
                to = slice(start - index * PADDED, stop - index * PADDED)
                target[to, :] = part.astype(target.dtype)


def scale_rows(part, gates, scaled, base):
    at = slice(base, base + part.shape[0])
    for cut in range(WIDTH // 128):
        lanes = slice(cut * 128, (cut + 1) * 128)
        scaled[at, lanes] = (part[:, lanes].astype(F32) * gates).astype(BF16)


def pair_grad_kernel(*refs):
    rights, lefts = refs[:5], refs[5:9]
    own_ref, low_ref, gates_ref, scaled = refs[9:]
    same = iota((ROWS, ROWS), 0) == iota((ROWS, ROWS), 1)
    ones = jnp.ones((ROWS, 128), BF16)
    for chunk in range(4):
        base = chunk * ROWS
        tile = rights[chunk][ROWS:, :ROWS] if chunk < 3 else rights[4][HALF:, :ROWS]
        gates = jnp.zeros((ROWS, 128), F32)
        for term in range(2):
            line = tile[term : term + 1, :].astype(F32)
            gates = gates + dot(jnp.where(same, line, 0.0).astype(BF16), ones)
        gates_ref[base : base + ROWS, :] = gates
        if chunk < 3:
            scale_rows(rights[chunk][:ROWS, :], gates, scaled, base)
        else:
            scale_rows(rights[3][...], gates[:HALF], scaled, base)
            scale_rows(rights[4][:HALF, :], gates[HALF:], scaled, base + HALF)
    put_weight_grads(lefts, scaled, [own_ref.at[0], own_ref.at[1], low_ref.at[0], low_ref.at[1]])


def down_grad_kernel(*refs):
    rights, lefts = refs[:4], refs[4:8]
    gates_ref, own_ref, low_ref, scaled = refs[8:]
    for chunk in range(4):
        at = slice(chunk * ROWS, (chunk + 1) * ROWS)
        scale_rows(rights[chunk][...], gates_ref[at, :], scaled, chunk * ROWS)
    put_weight_grads(lefts, scaled, [own_ref.at[0], low_ref.at[0]])


def assemble_kernel(core_ref, own_ref, got_ref, out_ref):
    core = core_ref[0]
    out_ref[core] = own_ref[...]
    out_ref[1 - core] = got_ref[...].astype(F32)


def halves_kernel(core_ref, pair_ref, down_ref, *outs):
    for which in range(2):
        expert = core_ref[which]
        pair_out, down_out = outs[2 * which : 2 * which + 2]
        zeros = jnp.zeros((PADDED - HIDDEN, WIDTH), BF16)
        for part in range(2):
            base = part * PADDED
            pair_out[base : base + HIDDEN, :] = pair_ref[expert, part].astype(BF16)
            pair_out[base + HIDDEN : base + PADDED, :] = zeros
        down_out[:HIDDEN, :] = down_ref[expert].astype(BF16)
        down_out[HIDDEN:, :] = zeros


def outer_sent_kernel(order_ref, heads_ref, low_ref, out_ref):
    for step in range(4):
        out_ref[step] = dot(heads_ref[order_ref[4 + step]], low_ref[...], TN).astype(BF16)


def outer_kept_kernel(order_ref, heads_ref, low_ref, got_ref, logit_ref, middle_ref, gain_ref, router_ref, *outs):
    for step, out in enumerate(outs):
        own = dot(heads_ref[order_ref[step]], low_ref[...], TN)
        out[...] = (own + got_ref[step].astype(F32)).astype(BF16)
    middle = middle_ref[...]
    scale = lax.rsqrt(jnp.mean(middle * middle, axis=-1, keepdims=True) + EPSILON)
    router_ref[...] = dot(logit_ref[...], middle * scale * gain_ref[...], TN, HIGHEST)


def fill_kernel(whole_hbm, *refs):
    parts, (out_hbm, total, sem) = refs[:4], refs[4:]
    total[...] = sum(p[...].astype(F32) for p in parts).astype(BF16)
    copy = pltpu.make_async_copy(total, out_hbm.at[384:512], sem)
    copy.start()
    copy.wait()


def fill(whole, parts):
    return pl.pallas_call(
        fill_kernel,
        out_shape=shape((512, WIDTH), BF16),
        in_specs=[HBM] + [VMEM] * 4,
        out_specs=HBM,
        scratch_shapes=[pltpu.VMEM((128, WIDTH), BF16), pltpu.SemaphoreType.DMA(())],
        input_output_aliases={0: 0},
        compiler_params=pltpu.CompilerParams(vmem_limit_bytes=24 << 20),
        cost_estimate=pl.CostEstimate(flops=100000000, bytes_accessed=0, transcendentals=0),
        name="fill",
    )(whole, *parts)


def kept_kernel(kept_ref, got_ref, *outs):
    for step, out in enumerate(outs):
        out[...] = (kept_ref[step].astype(F32) + got_ref[step].astype(F32)).astype(BF16)


def input_grad_kernel(own_ref, left_ref, right_ref, over_ref, tok_ref, gain_ref, middle_ref, out_ref):
    total = (own_ref[...].astype(F32) + left_ref[...].astype(F32)) + (
        right_ref[...].astype(F32) + over_ref[...].astype(F32)
    )
    inputs = tok_ref[...].astype(F32)
    scale = lax.rsqrt(jnp.mean(inputs * inputs, axis=-1, keepdims=True) + EPSILON)
    unit = inputs * scale
    weighted = total * gain_ref[...]
    out_ref[...] = middle_ref[...] + scale * (
        weighted - unit * jnp.mean(weighted * unit, axis=-1, keepdims=True)
    )


def share_kernel(parts_ref, out_ref):
    total = parts_ref[0].astype(F32)
    for index in range(1, 16):
        total = total + parts_ref[index].astype(F32)
    total = total.astype(BF16)
    for index in range(16):
        out_ref[index] = total


def finish_kernel(rows_ref, qkv_ref, out_ref):
    for c in range(3):
        for block in range(WIDTH // 128):
            cut = slice(block * 128, (block + 1) * 128)
            qkv_ref[c, cut, :] = rows_ref[c * 128 : (c + 1) * 128, cut].astype(F32).T
    out_ref[...] = rows_ref[384:512, :].astype(F32)


def on_device(
    tokens,
    layer_cotangent,
    attn_gain,
    qkv_weight,
    out_weight,
    rel_bias,
    moe_gain,
    router_weight,
    expert_in,
    expert_out,
    routes,
    buckets,
):
    narrow = lax.axis_index("narrow")
    core = lax.rem(narrow, 2)
    x = lax.div(narrow, 2)

    barrier = lax.optimization_barrier

    def shift(value, step):
        return lax.ppermute(value, "narrow", [(i, (i + 2 * step) % 8) for i in range(8)])

    def swap(value):
        return lax.ppermute(value, "narrow", [(i, i ^ 1) for i in range(8)])

    def flip(value, axis, mask):
        size = lax.axis_size(axis)
        return lax.ppermute(value, axis, [(i, i ^ mask) for i in range(size)])

    def sum_four(value, axis, unit):
        low = barrier(value.astype(BF16))
        parts = [low] + [flip(low, axis, mask * unit) for mask in (1, 2, 3)]
        parts = [p.astype(F32) for p in parts]
        return (parts[0] + parts[1]) + (parts[2] + parts[3])

    exchange_groups = [
        [w * 8 + chip * 2 + c for w in range(16) for c in range(2)] for chip in range(4)
    ]

    def exchange(value):
        return lax.all_to_all(
            value, ("wide", "narrow"), 0, 0, tiled=True, axis_index_groups=exchange_groups
        )

    def blocks(send):
        return exchange(send.reshape(EXPERTS, SLOTS, WIDTH)).reshape(EXPERTS * SLOTS, WIDTH)

    picks, place, cot_rows = call(
        spread_kernel,
        "spread",
        [
            shape((EXPERTS * SLOTS, TOK), BF16),
            shape((TOK, TOP), jnp.int32),
            shape((EXPERTS * SLOTS, WIDTH), BF16),
        ],
        [routes.T, routes, layer_cotangent],
    )
    cot_arrived = blocks(cot_rows)

    def everywhere(value):
        near = [value, shift(value, 1), shift(value, -1), shift(value, 2)]
        return near + [swap(v) for v in near]

    shards = everywhere(tokens)

    chips = [x, lax.rem(x + 3, 4), lax.rem(x + 1, 4), lax.rem(x + 2, 4)]
    order = jnp.stack([2 * c + core for c in chips] + [2 * c + (1 - core) for c in chips])
    order = order.astype(jnp.int32)
    bias = rel_bias.astype(BF16).astype(F32)
    offsets = jnp.pad(buckets, (0, 1), constant_values=-1)[None]
    backward_offsets = jnp.pad(buckets[::-1], (0, 1), constant_values=-1)[None]
    gain_one = attn_gain[None]
    gain_two = moe_gain[None]
    router_rows = router_weight.T
    wout_low, shards = barrier((out_weight.astype(BF16), shards))
    wouts = [wout_low, shift(wout_low, 1), shift(wout_low, -1), shift(wout_low, 2)]
    normed, qkv, attended, proj = attend_forward(
        order, bias, shards, gain_one, qkv_weight, offsets
    )
    attended, cot_arrived, wouts = barrier((attended, cot_arrived, wouts))
    wouts = wouts + [swap(w) for w in wouts]
    heads = lax.all_to_all(attended.reshape(8, TOK, 128), "narrow", 0, 0, tiled=True)
    cot_arrived, expert_in, expert_out = barrier((cot_arrived, expert_in, expert_out))

    pair, down, pair_other, down_other = call(
        halves_kernel,
        "halves",
        [shape((FULL, WIDTH), BF16), shape((PADDED, WIDTH), BF16)] * 2,
        [
            jnp.stack([core, 1 - core]).astype(jnp.int32),
            jnp.swapaxes(expert_in, 2, 3),
            expert_out,
        ],
        smem=1,
    )
    cot_arrived, pair = barrier((cot_arrived, pair))
    cot_own = unpack(cot_arrived, False)
    heads, pair, down, pair_other, down_other, cot_own = barrier(
        (heads, pair, down, pair_other, down_other, cot_own)
    )
    cot_parts = [cot_own, shift(cot_own, 1), shift(cot_own, -1), shift(cot_own, 2)]
    weights = [pair, swap(pair_other), down, swap(down_other)]
    middle, gates, send_rows, wout = call(
        dispatch_kernel,
        "dispatch",
        [
            shape((TOK, WIDTH), F32),
            shape((TOK, TOP), F32),
            shape((EXPERTS * SLOTS, WIDTH), BF16),
            shape((WIDTH, WIDTH), BF16),
        ],
        [order, heads, *wouts, tokens, gain_two, router_rows, routes, place, picks],
        smem=1,
    )

    arrived = blocks(send_rows)
    place, cot_parts = barrier((place, cot_parts))
    token_picks = call(
        slots_kernel,
        "slots",
        [shape((TOP, TOK, EXPERTS * SLOTS), BF16)],
        [routes, place],
    )[0]
    arrived, token_picks = barrier((arrived, token_picks))

    row_own = unpack(arrived, True)
    row_left, row_right = shift(row_own, 1), shift(row_own, -1)
    results = run_expert([([row_own], cot_parts[0])], weights)
    row_left, row_right, results = barrier((row_left, row_right, results))
    over = [shift(row_left[:HALF], 1), shift(row_right[HALF:], -1)]
    row_parts = [row_own, row_left, row_right]
    results += run_expert([([row_left], cot_parts[1]), ([row_right], cot_parts[2])], weights)
    over, results = barrier((over, results))
    row_parts = row_parts + over
    results += run_expert([(over, cot_parts[3])], weights)
    mids, inners = ([r[i] for r in results] for i in range(2))
    outs, backs = [r[2:4] for r in results], [r[4:6] for r in results]

    def leave_far(over):
        return [shift(over[0], -1), shift(over[1], 1)]

    def leave_near(left, right):
        return [shift(right[0], 1), shift(left[1], -1)]

    def land(own, left, right, near, far):
        left_top, right_end, part_top, part_end = join(*own, *near, left[0], far[0], right[1], far[1])
        return [part_top, part_end, left_top, right_end]

    def arrive(parts):
        return [parts[0], parts[1], shift(parts[2], -1), shift(parts[3], 1)]

    far, near = leave_far(backs[3]), leave_near(*backs[1:3])
    near, inners = barrier((near, inners))
    pair_part, pair_low, gate_columns = call(
        pair_grad_kernel,
        "pair_grad",
        [
            shape((2, HIDDEN, WIDTH), F32),
            shape((2, HIDDEN, WIDTH), BF16),
            shape((4 * ROWS, 128), F32),
        ],
        [*row_parts, *inners],
        [pltpu.VMEM((4 * ROWS, WIDTH), BF16)],
    )
    far, near, pair_part, pair_low = barrier((far, near, pair_part, pair_low))
    landed = land(*backs[:3], near, far)
    pair_part, landed = barrier((pair_part, landed))
    pair_grads = call(
        assemble_kernel,
        "assemble_pair",
        [shape((2, 2, HIDDEN, WIDTH), F32)],
        [core.astype(jnp.int32).reshape(1), pair_part, swap(pair_low)],
        smem=1,
    )[0]
    pieces, outs, mids, pair_grads = barrier((arrive(landed), outs, mids, pair_grads))
    out_far, out_near = leave_far(outs[3]), leave_near(*outs[1:3])
    back = call(collect_kernel, "collect", [shape((EXPERTS * SLOTS, WIDTH), BF16)], pieces)[0]
    row_grads = blocks(back)
    mids, out_far, out_near, _ = barrier((mids, out_far, out_near, back))
    out_parts = arrive(land(*outs[:3], out_near, out_far))
    down_part, down_low = call(
        down_grad_kernel,
        "down_grad",
        [shape((1, HIDDEN, WIDTH), F32), shape((1, HIDDEN, WIDTH), BF16)],
        [*cot_parts, *mids, gate_columns],
        [pltpu.VMEM((4 * ROWS, WIDTH), BF16)],
    )
    row_grads, down_part = barrier((row_grads, down_part))
    middle_grad, middle_low, send_heads, moe_gain_grad, logit_grads = call(
        middle_grad_kernel,
        "middle_grad",
        [
            shape((TOK, WIDTH), F32),
            shape((TOK, WIDTH), BF16),
            shape((8, TOK, 128), BF16),
            shape((1, WIDTH), F32),
            shape((TOK, EXPERTS), F32),
        ],
        [
            row_grads, gates, middle, layer_cotangent, routes, place, token_picks, gain_two,
            router_rows, wout,
        ],
    )
    head_grads = lax.all_to_all(send_heads, "narrow", 0, 0, tiled=True).reshape(LEN, 128)
    middle_low, out_parts = barrier((middle_low, out_parts))
    outer_sent = call(
        outer_sent_kernel,
        "outer_sent",
        [shape((4, 128, WIDTH), BF16)],
        [order, heads, middle_low],
        smem=1,
    )[0]
    back_out = call(collect_out_kernel, "collect_out", [shape((EXPERTS * SLOTS, WIDTH), BF16)], out_parts)[0]
    outer_got, head_grads, back_out = barrier((swap(outer_sent), head_grads, back_out))
    router_terms, *outer_parts = call(
        outer_kept_kernel,
        "outer_kept",
        [shape((EXPERTS, WIDTH), F32)] + [shape((128, WIDTH), BF16)] * 4,
        [order, heads, middle_low, outer_got, logit_grads, middle, gain_two],
        smem=1,
    )
    head_grads, back_out, outer_parts = barrier((head_grads, back_out, outer_parts))
    returned = blocks(back_out)

    def to_chips(parts):
        return [parts[0]] + [shift(p, step) for p, step in zip(parts[1:], (-1, 1, 2))]

    outer_parts = to_chips(outer_parts)
    bias_grad, weight_grads, gain_grad, sent, kept = attend_backward(
        order, bias, normed, qkv, attended, head_grads, backward_offsets, proj, gain_one
    )
    bias_grad, weight_grads, returned, outer_parts = barrier(
        (bias_grad, weight_grads, returned, outer_parts)
    )

    weight_grads = fill(weight_grads, outer_parts)
    arrived_grads = lax.all_to_all(weight_grads.reshape(16, 32, WIDTH), "wide", 0, 0, tiled=True)
    gain_grad, sent, _ = barrier((gain_grad, sent, weight_grads))

    small = sum_four(jnp.concatenate([router_terms, gain_grad, moe_gain_grad]), "narrow", 2)
    got, small, returned = barrier((swap(sent), small, returned))
    kept = call(
        kept_kernel,
        "kept",
        [shape((TOK, WIDTH), BF16)] * 4,
        [kept, got],
    )
    layer_out = call(
        combine_kernel,
        "combine",
        [shape((TOK, WIDTH), BF16)],
        [returned, middle, gates, token_picks],
    )[0]
    low = barrier(small.astype(BF16))
    small = low.astype(F32) + flip(low, "narrow", 1).astype(F32)
    small = jnp.concatenate(
        [small, jnp.pad(bias_grad.reshape(1, 64), ((0, 0), (0, WIDTH - 64)))]
    )
    arrived_grads, kept, layer_out = barrier((arrived_grads, kept, layer_out))
    copies = call(
        share_kernel, "share", [shape((16, 32, WIDTH), BF16)], [arrived_grads]
    )[0]
    gathered = lax.all_to_all(copies, "wide", 0, 0, tiled=True).reshape(512, WIDTH)
    small = sum_four(small, "wide", 1)
    chip_parts = to_chips(kept)
    down_part, small, chip_parts, _ = barrier((down_part, small, chip_parts, copies))
    down_grads = call(
        assemble_kernel,
        "assemble_down",
        [shape((2, 1, HIDDEN, WIDTH), F32)],
        [core.astype(jnp.int32).reshape(1), down_part, swap(down_low)],
        smem=1,
    )[0].reshape(2, HIDDEN, WIDTH)
    small = sum_four(small, "wide", 4)
    rel_bias_grad = small[EXPERTS + 2, : 2 * BUCKETS].reshape(2, BUCKETS)
    input_grad = call(
        input_grad_kernel,
        "input_grad",
        [shape((TOK, WIDTH), F32)],
        [*chip_parts, tokens, gain_one, middle_grad],
    )[0]
    qkv_weight_grad, out_weight_grad = call(
        finish_kernel,
        "finish",
        [shape((3, WIDTH, 128), F32), shape((128, WIDTH), F32)],
        [gathered],
    )
    return (
        layer_out,
        input_grad,
        small[EXPERTS],
        qkv_weight_grad,
        out_weight_grad,
        rel_bias_grad,
        small[EXPERTS + 1],
        small[:EXPERTS].T,
        jnp.swapaxes(pair_grads, 2, 3),
        down_grads,
    )


def solution(mesh):
    placed = (
        P(("wide", "narrow"), None),
        P(("wide", "narrow"), None),
        P(),
        P(None, None, "narrow"),
        P("narrow", None),
        P("narrow", None),
        P(),
        P(),
        P("wide", None, None, "narrow"),
        P("wide", "narrow", None),
        P(("wide", "narrow"), None),
        P(),
    )
    return jax.shard_map(
        on_device,
        mesh=mesh,
        in_specs=placed,
        out_specs=(
            P(("wide", "narrow"), None),
            P(("wide", "narrow"), None),
            P(),
            P(None, None, "narrow"),
            P("narrow", None),
            P("narrow", None),
            P(),
            P(),
            P("wide", None, None, "narrow"),
            P("wide", "narrow", None),
        ),
        check_vma=False,
    )
```

profile of v0, /device:TPU:1, one launch (start us, length us, event | category | flops | bytes accessed | tf_op | source)
XLA Modules:
  0.0 340.2 jit_solution(6624542110039353389)
XLA Ops:
  11.2 9.7 %all-to-all-start = ((bf16[32,16,1024]{2,1,0:T(8,128)(2,1)}), bf16[32,16,1024]{2,1,0:T(8,128)(2,1)S(1)}, u32[]{:S(2)}, u32[]{:S(2)}) async-start(bf16[32,16,1024]{2,1,0:T(8,128)(2,1)} %bitcast.10), calls=%async_computation | async-start | bytes 2097152 | tf_op jit(solution)/shard_map/all_to_all | solution.py:752
  29.4 11.4 %attend_forward.1 = (bf16[1408,1024]{1,0:T(8,128)(2,1)S(1)}, bf16[1408,512]{1,0:T(8,128)(2,1)S(1)}, bf16[1408,128]{1,0:T(8,128)(2,1)}, bf16[384,1024]{1,0:T(8,128)(2,1)S(1)}) custom-call(s32[8]{0:T(128)S(1)} %stack.44.place_ref.order_ref, f32[2,32]{1,0:T(2,128)S(1)} %convert_convert_fusion.bias_ref, bf16[176,1024]{1,0:T(8,128)(2,1)S(1)} %copy-done.24, ...), custom_call_target="tpu_custom_call" | custom-call | flops 4600000000 | tf_op jit(solution)/shard_map/attend_forward/pallas_call | solution.py:75
  46.0 5.3 %all-to-all-start.1 = ((bf16[8,176,128]{2,1,0:T(8,128)(2,1)}), bf16[8,176,128]{2,1,0:T(8,128)(2,1)S(1)}, u32[]{:S(2)}, u32[]{:S(2)}) async-start(bf16[8,176,128]{2,1,0:T(8,128)(2,1)} %bitcast.12), calls=%async_computation.1 | async-start | bytes 720896 | tf_op jit(solution)/shard_map/all_to_all | solution.py:793
  52.3 6.1 %halves.1 = (bf16[768,1024]{1,0:T(8,128)(2,1)}, bf16[384,1024]{1,0:T(8,128)(2,1)}, bf16[768,1024]{1,0:T(8,128)(2,1)}, bf16[384,1024]{1,0:T(8,128)(2,1)}) custom-call(s32[2]{0:T(128)} %pad_add_fusion.core_ref, f32[2,2,352,1024]{3,2,1,0:T(8,128)} %bitcast.53, f32[2,352,1024]{2,1,0:T(8,128)} %down_ref), custom_call_target="tpu_custom_call" | custom-call | flops 57500000256 | tf_op jit(solution)/shard_map/halves/pallas_call | solution.py:75
  63.7 5.6 %dispatch.1 = (f32[176,1024]{1,0:T(8,128)}, f32[176,2]{1,0:T(8,128)}, bf16[512,1024]{1,0:T(8,128)(2,1)}, bf16[1024,1024]{1,0:T(8,128)(2,1)}) custom-call(s32[8]{0:T(128)} %copy-done.32, bf16[8,176,128]{2,1,0:T(8,128)(2,1)} %copy-done.3, bf16[128,1024]{1,0:T(8,128)(2,1)} %convert_element_type.63.refs_0_, bf16[128,1024]{1,0:T(8,128)(2,1)} %copy-done.61, ...), custom_call_target="tpu_custom_call" | custom-call | flops 57500000256 | tf_op jit(solution)/shard_map/dispatch/pallas_call | solution.py:75
  69.3 9.4 %all-to-all-start.2 = ((bf16[32,16,1024]{2,1,0:T(8,128)(2,1)}), bf16[32,16,1024]{2,1,0:T(8,128)(2,1)S(1)}, u32[]{:S(2)}, u32[]{:S(2)}) async-start(bf16[32,16,1024]{2,1,0:T(8,128)(2,1)} %bitcast.47), calls=%async_computation.2 | async-start | bytes 2097152 | tf_op jit(solution)/shard_map/all_to_all | solution.py:752
  80.7 19.5 %collective-permute-done.16.refs_2_.refs_3_ = bf16[416,1024]{1,0:T(8,128)(2,1)} collective-permute-done((bf16[416,1024]{1,0:T(8,128)(2,1)S(1)}, bf16[416,1024]{1,0:T(8,128)(2,1)}, u32[]{:S(2)}, u32[]{:S(2)}) %collective-permute-start.16) | collective-permute-done | bytes 852000 | tf_op jit(solution)/shard_map/ppermute | solution.py:732
  105.9 6.6 %expert.3 = (bf16[416,768]{1,0:T(8,128)(2,1)S(1)}, bf16[416,1536]{1,0:T(8,128)(2,1)S(1)}, bf16[208,1024]{1,0:T(8,128)(2,1)S(1)}, bf16[208,1024]{1,0:T(8,128)(2,1...) custom-call(bf16[432,1024]{1,0:T(8,128)(2,1)S(1)} %unpack.3.refs_0_, ...), custom_call_target="tpu_custom_call" | custom-call | flops 57500000256 | tf_op jit(solution)/shard_map/expert/pallas_call | solution.py:75
  113.4 9.8 %collective-permute-done.17.refs_0_.refs_1_ = bf16[432,1024]{1,0:T(8,128)(2,1)S(1)} collective-permute-done((bf16[432,1024]{1,0:T(8,128)(2,1)S(1)}, bf16[432,1024]{1,0:T(8,128)(2,1)S(1)}, u32[]{:S(2)}, u32[]{:S(2)}) %collective-permute-start.17) | collective-permute-done | bytes 884768 | tf_op jit(solution)/shard_map/ppermute | solution.py:732
  123.4 3.1 collective-permute-start.22
  126.6 12.1 %expert.4 = (bf16[416,768]{1,0:T(8,128)(2,1)S(1)}, bf16[416,1536]{1,0:T(8,128)(2,1)S(1)}, bf16[208,1024]{1,0:T(8,128)(2,1)S(1)}, bf16[208,1024]{1,0:T(8,128)(2,1...) custom-call(bf16[432,1024]{1,0:T(8,128)(2,1)S(1)} %collective-permut, ...), custom_call_target="tpu_custom_call" | custom-call | flops 57500000256 | tf_op jit(solution)/shard_map/expert/pallas_call | solution.py:75
  141.5 2.8 collective-permute-start.26
  144.3 7.7 %expert.5 = (bf16[416,768]{1,0:T(8,128)(2,1)S(1)}, bf16[416,1536]{1,0:T(8,128)(2,1)S(1)}, bf16[208,1024]{1,0:T(8,128)(2,1)}, bf16[208,1024]{1,0:T(8,128)(2,1)}, ...) custom-call(bf16[208,1024]{1,0:T(8,128)(2,1)S(1)} %collective-permute-done.21.refs_0_.refs_3_, ...), custom_call_target="tpu_custom_call" | custom-call | flops 57500000256 | tf_op jit(solution)/shard_map/expert/pallas_call | solution.py:75
  154.7 7.7 %pair_grad.1 = (f32[2,352,1024]{2,1,0:T(8,128)S(1)}, bf16[2,352,1024]{2,1,0:T(8,128)(2,1)S(1)}, f32[1664,128]{1,0:T(8,128)S(1)}) custom-call(bf16[432,1024]{1,0:T(8,128)(2,1)S(1)} %unpack.3.refs_0_, bf16[432,1024]{1,0:T(8,128)(2,1)S(1)} %collective-permute-done.17.refs_0_.refs_1_, bf16[432,1024]{1,0:T(8,128)(2,1)S(1)} %collective-permute-done.18.refs_2_, ...), custom_call_target="tpu_custom_call" | custom-call | flops 3449999872 | tf_op jit(solution)/shard_map/pair_grad/pallas_call | solution.py:75
  164.0 3.9 %collective-permute-start.29 = (bf16[2,352,1024]{2,1,0:T(8,128)(2,1)S(1)}, bf16[2,352,1024]{2,1,0:T(8,128)(2,1)S(1)}, u32[]{:S(2)}, u32[]{:S(2)}) collective-permute-start(bf16[2,352,1024]{2,1,0:T(8,128)(2,1)S(1)} %get-tuple-element.343), channel_id=1, source_target_pairs={{0,1},{1,0},{2,3},{3,2},{4,5},{5,4},{6,7},{7,6},{8,9},{9,8},{10,11... | collective-permute-start | bytes 4325384 | tf_op jit(solution)/shard_map/ppermute | solution.py:735
  172.5 5.1 %assemble_pair.1 = f32[2,2,352,1024]{3,2,1,0:T(8,128)} custom-call(s32[1]{0:T(128)} %bitcast.13.core_ref, f32[2,352,1024]{2,1,0:T(8,128)} %copy-done.5, bf16[2,352,1024]{2,1,0:T(8,128)(2,1)} %copy-done.55), custom_call_target="tpu_custom_call" | custom-call | flops 115000000 | tf_op jit(solution)/shard_map/assemble_pair/pallas_call | solution.py:75
  183.4 2.7 collective-permute-start.33
  188.1 10.5 %all-to-all-start.3 = ((bf16[32,16,1024]{2,1,0:T(8,128)(2,1)}), bf16[32,16,1024]{2,1,0:T(8,128)(2,1)}, u32[]{:S(2)}, u32[]{:S(2)}) async-start(bf16[32,16,1024]{2,1,0:T(8,128)(2,1)} %bitcast.20), calls=%async_computation.3 | async-start | bytes 2097152 | tf_op jit(solution)/shard_map/all_to_all | solution.py:752
  198.6 4.9 %collective-permute-done.32.near_top = bf16[208,1024]{1,0:T(8,128)(2,1)S(1)} collective-permute-done((bf16[208,1024]{1,0:T(8,128)(2,1)}, bf16[208,1024]{1,0:T(8,128)(2,1)S(1)}, u32[]{:S(2)}, u32[]{:S(2)}) %collective-permute-start.32) | collective-permute-done | bytes 426016 | tf_op jit(solution)/shard_map/ppermute | solution.py:732
  208.1 7.4 %down_grad.1 = (f32[1,352,1024]{2,1,0:T(8,128)}, bf16[1,352,1024]{2,1,0:T(8,128)(2,1)}) custom-call(bf16[416,1024]{1,0:T(8,128)(2,1)} %copy-done.16, bf16[416,1024]{1,0:T(8,128)(2,1)} %copy-done.38, bf16[416,1024]{1,0:T(8,128)(2,1)} %collective-permute-done.15.refs_3_.refs_2_, bf16[416,1024]{1,0:T(8,128)(2,1)} %collective-permute-done.16.refs_2_.refs_3_, ...), custom_call_target="tpu_custom_call" | custom-call | flops 57500000256 | tf_op jit(solution)/shard_map/down_grad/pallas_call | solution.py:75
  215.8 6.0 %middle_grad.1 = (f32[176,1024]{1,0:T(8,128)}, bf16[176,1024]{1,0:T(8,128)(2,1)}, bf16[8,176,128]{2,1,0:T(8,128)(2,1)}, f32[1,1024]{1,0:T(1,128)}, f32[176,32]{1,0:T(8,128)}) custom-call(bf16[512,1024]{1,0:T(8,128)(2,1)} %bitcast.21.rows_ref, f32[176,2]{1,0:T(8,128)} %get-tuple-element.363.gates_ref, f32[176,1024]{1,0:T(8,128)} %get-tuple-element.364.middle_ref, ...), custom_call_target="tpu_custom_call" | custom-call | flops 115000000 | tf_op jit(solution)/shard_map/middle_grad/pallas_call | solution.py:75
  224.7 2.9 collective-permute-start.36
  227.6 4.2 %all-to-all-start.4 = ((bf16[8,176,128]{2,1,0:T(8,128)(2,1)}), bf16[8,176,128]{2,1,0:T(8,128)(2,1)}, u32[]{:S(2)}, u32[]{:S(2)}) async-start(bf16[8,176,128]{2,1,0:T(8,128)(2,1)} %get-tuple-element.381), calls=%async_computation.4 | async-start | bytes 720896 | tf_op jit(solution)/shard_map/all_to_all | solution.py:915
  243.0 9.0 %all-to-all-start.5 = ((bf16[32,16,1024]{2,1,0:T(8,128)(2,1)}), bf16[32,16,1024]{2,1,0:T(8,128)(2,1)S(1)}, u32[]{:S(2)}, u32[]{:S(2)}) async-start(bf16[32,16,1024]{2,1,0:T(8,128)(2,1)} %bitcast.23), calls=%async_computation.5 | async-start | bytes 2097152 | tf_op jit(solution)/shard_map/all_to_all | solution.py:752
  255.0 21.9 %attend_backward.1 = (f32[2,32]{1,0:T(2,128)}, bf16[512,1024]{1,0:T(8,128)(2,1)}, f32[1,1024]{1,0:T(1,128)}, bf16[4,176,1024]{2,1,0:T(8,128)(2,1)}, bf16[4,176,1024]{2,1,0:T(8,128)(2,1)}) custom-call(s32[8]{0:T(128)} %copy-done.32, f32[2,32]{1,0:T(2,128)} %copy-done.36, bf16[1408,1024]{1,0:T(8,128)(2,1)} %copy-done.44, bf16[1408,512]{1,0:T(8,128)(2,1)} %copy-done.45, ...), custom_call_target="tpu_custom_call" | custom-call | flops 57500000256 | tf_op jit(solution)/shard_map/attend_backward/pallas_call | solution.py:75
  280.4 6.9 %all-to-all-start.6 = ((bf16[16,32,1024]{2,1,0:T(8,128)(2,1)}), bf16[16,32,1024]{2,1,0:T(8,128)(2,1)S(1)}, u32[]{:S(2)}, u32[]{:S(2)}) async-start(bf16[16,32,1024]{2,1,0:T(8,128)(2,1)} %bitcast.34), calls=%async_computation.6 | async-start | bytes 2097152 | tf_op jit(solution)/shard_map/all_to_all | solution.py:948
  297.8 2.9 collective-permute-start.47
  310.3 6.7 %all-to-all-start.7 = ((bf16[16,32,1024]{2,1,0:T(8,128)(2,1)}), bf16[16,32,1024]{2,1,0:T(8,128)(2,1)S(1)}, u32[]{:S(2)}, u32[]{:S(2)}) async-start(bf16[16,32,1024]{2,1,0:T(8,128)(2,1)} %share.1), calls=%async_computation.7 | async-start | bytes 2097152 | tf_op jit(solution)/shard_map/all_to_all | solution.py:974
  318.8 6.1 %collective-permute-done.50.over_ref = bf16[176,1024]{1,0:T(8,128)(2,1)S(1)} collective-permute-done((bf16[176,1024]{1,0:T(8,128)(2,1)}, bf16[176,1024]{1,0:T(8,128)(2,1)S(1)}, u32[]{:S(2)}, u32[]{:S(2)}) %collective-permute-start.50) | collective-permute-done | bytes 360480 | tf_op jit(solution)/shard_map/ppermute | solution.py:732
  324.9 3.6 %collective-permute-start.53 = (bf16[35,1024]{1,0:T(8,128)(2,1)S(1)}, bf16[35,1024]{1,0:T(8,128)(2,1)S(1)}, u32[]{:S(2)}, u32[]{:S(2)}) collective-permute-start(bf16[35,1024]{1,0:T(8,128)(2,1)S(1)} %add_add_fusion.1), channel_id=1, source_target_pairs={{0,96},{8,104},{16,112},{24,120},{32,64},{40,72},{48,80},{56,88},{... | collective-permute-start | bytes 215048 | tf_op jit(solution)/shard_map/ppermute | solution.py:739
  329.0 3.3 assemble_down.1
  333.7 2.7 collective-permute-done.53
  (280 shorter events, 111.1 us)
Async XLA Ops:
  0.6 20.6 %collective-permute-start = (bf16[176,1024]{1,0:T(8,128)(2,1)}, bf16[176,1024]{1,0:T(8,128)(2,1)S(1)}, u32[]{:S(2)}, u32[]{:S(2)}) collective-permute-start(bf16[176,1024]{1,0:T(8,128)(2,1)} %tok_ref.1), channel_id=1, source_target_pairs={{0,2},{1,3},{2,4},{3,5},{4,6},{5,7},{6,0},{7,1},{8,10},{9,11},{10,... | collective-permute-start | bytes 1081352 | tf_op jit(solution)/shard_map/ppermute | solution.py:732
  2.8 18.8 %collective-permute-start.1 = (bf16[176,1024]{1,0:T(8,128)(2,1)}, bf16[176,1024]{1,0:T(8,128)(2,1)S(1)}, u32[]{:S(2)}, u32[]{:S(2)}) collective-permute-start(bf16[176,1024]{1,0:T(8,128)(2,1)} %tok_ref.1), channel_id=1, source_target_pairs={{0,6},{1,7},{2,0},{3,1},{4,2},{5,3},{6,4},{7,5},{8,14},{9,15},{10,... | collective-permute-start | bytes 1081352 | tf_op jit(solution)/shard_map/ppermute | solution.py:732
  4.1 17.7 %collective-permute-start.2 = (bf16[176,1024]{1,0:T(8,128)(2,1)}, bf16[176,1024]{1,0:T(8,128)(2,1)S(1)}, u32[]{:S(2)}, u32[]{:S(2)}) collective-permute-start(bf16[176,1024]{1,0:T(8,128)(2,1)} %tok_ref.1), channel_id=1, source_target_pairs={{0,4},{1,5},{2,6},{3,7},{4,0},{5,1},{6,2},{7,3},{8,12},{9,13},{10,... | collective-permute-start | bytes 1081352 | tf_op jit(solution)/shard_map/ppermute | solution.py:732
  11.2 34.8 %all-to-all-start = ((bf16[32,16,1024]{2,1,0:T(8,128)(2,1)}), bf16[32,16,1024]{2,1,0:T(8,128)(2,1)S(1)}, u32[]{:S(2)}, u32[]{:S(2)}) async-start(bf16[32,16,1024]{2,1,0:T(8,128)(2,1)} %bitcast.10), calls=%async_computation | async-start | bytes 2097152 | tf_op jit(solution)/shard_map/all_to_all | solution.py:752
  25.0 19.5 %collective-permute-start.7 = (bf16[128,1024]{1,0:T(8,128)(2,1)}, bf16[128,1024]{1,0:T(8,128)(2,1)S(1)}, u32[]{:S(2)}, u32[]{:S(2)}) collective-permute-start(bf16[128,1024]{1,0:T(8,128)(2,1)} %convert_element_type.63.refs_0_), channel_id=1, source_target_pairs={{0,2},{1,3},{2,4},{3,5},{4,6},{5,7},{6,0},{7,1},{8,10},{9,11},{10,... | collective-permute-start | bytes 786440 | tf_op jit(solution)/shard_map/ppermute | solution.py:732
  26.0 18.6 %collective-permute-start.8 = (bf16[128,1024]{1,0:T(8,128)(2,1)}, bf16[128,1024]{1,0:T(8,128)(2,1)S(1)}, u32[]{:S(2)}, u32[]{:S(2)}) collective-permute-start(bf16[128,1024]{1,0:T(8,128)(2,1)} %convert_element_type.63.refs_0_), channel_id=1, source_target_pairs={{0,6},{1,7},{2,0},{3,1},{4,2},{5,3},{6,4},{7,5},{8,14},{9,15},{10,... | collective-permute-start | bytes 786440 | tf_op jit(solution)/shard_map/ppermute | solution.py:732
  27.8 18.2 %collective-permute-start.9 = (bf16[128,1024]{1,0:T(8,128)(2,1)}, bf16[128,1024]{1,0:T(8,128)(2,1)}, u32[]{:S(2)}, u32[]{:S(2)}) collective-permute-start(bf16[128,1024]{1,0:T(8,128)(2,1)} %convert_element_type.63.refs_0_), channel_id=1, source_target_pairs={{0,4},{1,5},{2,6},{3,7},{4,0},{5,1},{6,2},{7,3},{8,12},{9,13},{10,... | collective-permute-start | bytes 786440 | tf_op jit(solution)/shard_map/ppermute | solution.py:732
  59.1 21.3 %collective-permute-start.14 = (bf16[416,1024]{1,0:T(8,128)(2,1)S(1)}, bf16[416,1024]{1,0:T(8,128)(2,1)S(1)}, u32[]{:S(2)}, u32[]{:S(2)}) collective-permute-start(bf16[416,1024]{1,0:T(8,128)(2,1)S(1)} %unpack.2.refs_1_.refs_0_), channel_id=1, source_target_pairs={{0,2},{1,3},{2,4},{3,5},{4,6},{5,7},{6,0},{7,1},{8,10},{9,11},{10,... | collective-permute-start | bytes 2555912 | tf_op jit(solution)/shard_map/ppermute | solution.py:732
  60.7 20.0 %collective-permute-start.15 = (bf16[416,1024]{1,0:T(8,128)(2,1)S(1)}, bf16[416,1024]{1,0:T(8,128)(2,1)}, u32[]{:S(2)}, u32[]{:S(2)}) collective-permute-start(bf16[416,1024]{1,0:T(8,128)(2,1)S(1)} %unpack.2.refs_1_.refs_0_), channel_id=1, source_target_pairs={{0,6},{1,7},{2,0},{3,1},{4,2},{5,3},{6,4},{7,5},{8,14},{9,15},{10,... | collective-permute-start | bytes 2555912 | tf_op jit(solution)/shard_map/ppermute | solution.py:732
  62.1 38.1 %collective-permute-start.16 = (bf16[416,1024]{1,0:T(8,128)(2,1)S(1)}, bf16[416,1024]{1,0:T(8,128)(2,1)}, u32[]{:S(2)}, u32[]{:S(2)}) collective-permute-start(bf16[416,1024]{1,0:T(8,128)(2,1)S(1)} %unpack.2.refs_1_.refs_0_), channel_id=1, source_target_pairs={{0,4},{1,5},{2,6},{3,7},{4,0},{5,1},{6,2},{7,3},{8,12},{9,13},{10,... | collective-permute-start | bytes 2555912 | tf_op jit(solution)/shard_map/ppermute | solution.py:732
  69.3 31.8 %all-to-all-start.2 = ((bf16[32,16,1024]{2,1,0:T(8,128)(2,1)}), bf16[32,16,1024]{2,1,0:T(8,128)(2,1)S(1)}, u32[]{:S(2)}, u32[]{:S(2)}) async-start(bf16[32,16,1024]{2,1,0:T(8,128)(2,1)} %bitcast.47), calls=%async_computation.2 | async-start | bytes 2097152 | tf_op jit(solution)/shard_map/all_to_all | solution.py:752
  78.8 26.0 %collective-permute-start.19 = (bf16[768,1024]{1,0:T(8,128)(2,1)}, bf16[768,1024]{1,0:T(8,128)(2,1)}, u32[]{:S(2)}, u32[]{:S(2)}) collective-permute-start(bf16[768,1024]{1,0:T(8,128)(2,1)} %get-tuple-element.263), channel_id=1, source_target_pairs={{0,1},{1,0},{2,3},{3,2},{4,5},{5,4},{6,7},{7,6},{8,9},{9,8},{10,11... | collective-permute-start | bytes 4718600 | tf_op jit(solution)/shard_map/ppermute | solution.py:735
  79.1 25.7 %collective-permute-start.20 = (bf16[384,1024]{1,0:T(8,128)(2,1)}, bf16[384,1024]{1,0:T(8,128)(2,1)}, u32[]{:S(2)}, u32[]{:S(2)}) collective-permute-start(bf16[384,1024]{1,0:T(8,128)(2,1)} %get-tuple-element.265), channel_id=1, source_target_pairs={{0,1},{1,0},{2,3},{3,2},{4,5},{5,4},{6,7},{7,6},{8,9},{9,8},{10,11... | collective-permute-start | bytes 2359304 | tf_op jit(solution)/shard_map/ppermute | solution.py:735
  102.0 21.2 %collective-permute-start.17 = (bf16[432,1024]{1,0:T(8,128)(2,1)S(1)}, bf16[432,1024]{1,0:T(8,128)(2,1)S(1)}, u32[]{:S(2)}, u32[]{:S(2)}) collective-permute-start(bf16[432,1024]{1,0:T(8,128)(2,1)S(1)} %unpack.3.refs_0_), channel_id=1, source_target_pairs={{0,2},{1,3},{2,4},{3,5},{4,6},{5,7},{6,0},{7,1},{8,10},{9,11},{10,... | collective-permute-start | bytes 2654216 | tf_op jit(solution)/shard_map/ppermute | solution.py:732
  102.6 20.6 %collective-permute-start.18 = (bf16[432,1024]{1,0:T(8,128)(2,1)S(1)}, bf16[432,1024]{1,0:T(8,128)(2,1)S(1)}, u32[]{:S(2)}, u32[]{:S(2)}) collective-permute-start(bf16[432,1024]{1,0:T(8,128)(2,1)S(1)} %unpack.3.refs_0_), channel_id=1, source_target_pairs={{0,6},{1,7},{2,0},{3,1},{4,2},{5,3},{6,4},{7,5},{8,14},{9,15},{10,... | collective-permute-start | bytes 2654216 | tf_op jit(solution)/shard_map/ppermute | solution.py:732
  123.3 18.1 %collective-permute-start.21 = (bf16[208,1024]{1,0:T(8,128)(2,1)S(1)}, bf16[208,1024]{1,0:T(8,128)(2,1)S(1)}, u32[]{:S(2)}, u32[]{:S(2)}) collective-permute-start(bf16[208,1024]{1,0:T(8,128)(2,1)S(1)} %slice.18), channel_id=1, source_target_pairs={{0,2},{1,3},{2,4},{3,5},{4,6},{5,7},{6,0},{7,1},{8,10},{9,11},{10,... | collective-permute-start | bytes 1277960 | tf_op jit(solution)/shard_map/ppermute | solution.py:732
  123.4 18.0 %collective-permute-start.22 = (bf16[224,1024]{1,0:T(8,128)(2,1)S(1)}, bf16[224,1024]{1,0:T(8,128)(2,1)S(1)}, u32[]{:S(2)}, u32[]{:S(2)}) collective-permute-start(bf16[224,1024]{1,0:T(8,128)(2,1)S(1)} %slice.19), channel_id=1, source_target_pairs={{0,6},{1,7},{2,0},{3,1},{4,2},{5,3},{6,4},{7,5},{8,14},{9,15},{10,... | collective-permute-start | bytes 1376264 | tf_op jit(solution)/shard_map/ppermute | solution.py:732
  181.7 16.9 %collective-permute-start.30 = (bf16[208,1024]{1,0:T(8,128)(2,1)}, bf16[208,1024]{1,0:T(8,128)(2,1)S(1)}, u32[]{:S(2)}, u32[]{:S(2)}) collective-permute-start(bf16[208,1024]{1,0:T(8,128)(2,1)} %get-tuple-element.352), channel_id=1, source_target_pairs={{0,6},{1,7},{2,0},{3,1},{4,2},{5,3},{6,4},{7,5},{8,14},{9,15},{10,... | collective-permute-start | bytes 1277960 | tf_op jit(solution)/shard_map/ppermute | solution.py:732
  183.4 15.3 %collective-permute-start.31 = (bf16[208,1024]{1,0:T(8,128)(2,1)}, bf16[208,1024]{1,0:T(8,128)(2,1)S(1)}, u32[]{:S(2)}, u32[]{:S(2)}) collective-permute-start(bf16[208,1024]{1,0:T(8,128)(2,1)} %get-tuple-element.353), channel_id=1, source_target_pairs={{0,2},{1,3},{2,4},{3,5},{4,6},{5,7},{6,0},{7,1},{8,10},{9,11},{10,... | collective-permute-start | bytes 1277960 | tf_op jit(solution)/shard_map/ppermute | solution.py:732
  183.4 20.2 %collective-permute-start.32 = (bf16[208,1024]{1,0:T(8,128)(2,1)}, bf16[208,1024]{1,0:T(8,128)(2,1)S(1)}, u32[]{:S(2)}, u32[]{:S(2)}) collective-permute-start(bf16[208,1024]{1,0:T(8,128)(2,1)} %get-tuple-element.354), channel_id=1, source_target_pairs={{0,2},{1,3},{2,4},{3,5},{4,6},{5,7},{6,0},{7,1},{8,10},{9,11},{10,... | collective-permute-start | bytes 1277960 | tf_op jit(solution)/shard_map/ppermute | solution.py:732
  183.4 20.2 %collective-permute-start.33 = (bf16[208,1024]{1,0:T(8,128)(2,1)}, bf16[208,1024]{1,0:T(8,128)(2,1)S(1)}, u32[]{:S(2)}, u32[]{:S(2)}) collective-permute-start(bf16[208,1024]{1,0:T(8,128)(2,1)} %get-tuple-element.355), channel_id=1, source_target_pairs={{0,6},{1,7},{2,0},{3,1},{4,2},{5,3},{6,4},{7,5},{8,14},{9,15},{10,... | collective-permute-start | bytes 1277960 | tf_op jit(solution)/shard_map/ppermute | solution.py:732
  188.1 27.7 %all-to-all-start.3 = ((bf16[32,16,1024]{2,1,0:T(8,128)(2,1)}), bf16[32,16,1024]{2,1,0:T(8,128)(2,1)}, u32[]{:S(2)}, u32[]{:S(2)}) async-start(bf16[32,16,1024]{2,1,0:T(8,128)(2,1)} %bitcast.20), calls=%async_computation.3 | async-start | bytes 2097152 | tf_op jit(solution)/shard_map/all_to_all | solution.py:752
  206.6 15.2 %collective-permute-start.34 = (bf16[208,1024]{1,0:T(8,128)(2,1)}, bf16[208,1024]{1,0:T(8,128)(2,1)S(1)}, u32[]{:S(2)}, u32[]{:S(2)}) collective-permute-start(bf16[208,1024]{1,0:T(8,128)(2,1)} %get-tuple-element.378), channel_id=1, source_target_pairs={{0,6},{1,7},{2,0},{3,1},{4,2},{5,3},{6,4},{7,5},{8,14},{9,15},{10,... | collective-permute-start | bytes 1277960 | tf_op jit(solution)/shard_map/ppermute | solution.py:732
  243.0 33.9 %all-to-all-start.5 = ((bf16[32,16,1024]{2,1,0:T(8,128)(2,1)}), bf16[32,16,1024]{2,1,0:T(8,128)(2,1)S(1)}, u32[]{:S(2)}, u32[]{:S(2)}) async-start(bf16[32,16,1024]{2,1,0:T(8,128)(2,1)} %bitcast.23), calls=%async_computation.5 | async-start | bytes 2097152 | tf_op jit(solution)/shard_map/all_to_all | solution.py:752
  252.0 24.9 %collective-permute-start.37 = (bf16[128,1024]{1,0:T(8,128)(2,1)}, bf16[128,1024]{1,0:T(8,128)(2,1)S(1)}, u32[]{:S(2)}, u32[]{:S(2)}) collective-permute-start(bf16[128,1024]{1,0:T(8,128)(2,1)} %get-tuple-element.400), channel_id=1, source_target_pairs={{0,6},{1,7},{2,0},{3,1},{4,2},{5,3},{6,4},{7,5},{8,14},{9,15},{10,... | collective-permute-start | bytes 786440 | tf_op jit(solution)/shard_map/ppermute | solution.py:732
  253.2 23.6 %collective-permute-start.38 = (bf16[128,1024]{1,0:T(8,128)(2,1)}, bf16[128,1024]{1,0:T(8,128)(2,1)S(1)}, u32[]{:S(2)}, u32[]{:S(2)}) collective-permute-start(bf16[128,1024]{1,0:T(8,128)(2,1)} %get-tuple-element.401), channel_id=1, source_target_pairs={{0,2},{1,3},{2,4},{3,5},{4,6},{5,7},{6,0},{7,1},{8,10},{9,11},{10,... | collective-permute-start | bytes 786440 | tf_op jit(solution)/shard_map/ppermute | solution.py:732
  253.5 23.4 %collective-permute-start.39 = (bf16[128,1024]{1,0:T(8,128)(2,1)}, bf16[128,1024]{1,0:T(8,128)(2,1)S(1)}, u32[]{:S(2)}, u32[]{:S(2)}) collective-permute-start(bf16[128,1024]{1,0:T(8,128)(2,1)} %copy-done.40), channel_id=1, source_target_pairs={{0,4},{1,5},{2,6},{3,7},{4,0},{5,1},{6,2},{7,3},{8,12},{9,13},{10,... | collective-permute-start | bytes 786440 | tf_op jit(solution)/shard_map/ppermute | solution.py:732
  279.3 15.6 %collective-permute-start.40 = (bf16[4,176,1024]{2,1,0:T(8,128)(2,1)}, bf16[4,176,1024]{2,1,0:T(8,128)(2,1)}, u32[]{:S(2)}, u32[]{:S(2)}) collective-permute-start(bf16[4,176,1024]{2,1,0:T(8,128)(2,1)} %get-tuple-element.411), channel_id=1, source_target_pairs={{0,1},{1,0},{2,3},{3,2},{4,5},{5,4},{6,7},{7,6},{8,9},{9,8},{10,11... | collective-permute-start | bytes 4325384 | tf_op jit(solution)/shard_map/ppermute | solution.py:735
  280.4 25.5 %all-to-all-start.6 = ((bf16[16,32,1024]{2,1,0:T(8,128)(2,1)}), bf16[16,32,1024]{2,1,0:T(8,128)(2,1)S(1)}, u32[]{:S(2)}, u32[]{:S(2)}) async-start(bf16[16,32,1024]{2,1,0:T(8,128)(2,1)} %bitcast.34), calls=%async_computation.6 | async-start | bytes 2097152 | tf_op jit(solution)/shard_map/all_to_all | solution.py:948
  301.3 27.8 %collective-permute-start.54 = (bf16[1,352,1024]{2,1,0:T(8,128)(2,1)}, bf16[1,352,1024]{2,1,0:T(8,128)(2,1)}, u32[]{:S(2)}, u32[]{:S(2)}) collective-permute-start(bf16[1,352,1024]{2,1,0:T(8,128)(2,1)} %get-tuple-element.441), channel_id=1, source_target_pairs={{0,1},{1,0},{2,3},{3,2},{4,5},{5,4},{6,7},{7,6},{8,9},{9,8},{10,11... | collective-permute-start | bytes 2162696 | tf_op jit(solution)/shard_map/ppermute | solution.py:735
  307.4 17.5 %collective-permute-start.50 = (bf16[176,1024]{1,0:T(8,128)(2,1)}, bf16[176,1024]{1,0:T(8,128)(2,1)S(1)}, u32[]{:S(2)}, u32[]{:S(2)}) collective-permute-start(bf16[176,1024]{1,0:T(8,128)(2,1)} %get-tuple-element.429), channel_id=1, source_target_pairs={{0,4},{1,5},{2,6},{3,7},{4,0},{5,1},{6,2},{7,3},{8,12},{9,13},{10,... | collective-permute-start | bytes 1081352 | tf_op jit(solution)/shard_map/ppermute | solution.py:732
  310.3 28.1 %all-to-all-start.7 = ((bf16[16,32,1024]{2,1,0:T(8,128)(2,1)}), bf16[16,32,1024]{2,1,0:T(8,128)(2,1)S(1)}, u32[]{:S(2)}, u32[]{:S(2)}) async-start(bf16[16,32,1024]{2,1,0:T(8,128)(2,1)} %share.1), calls=%async_computation.7 | async-start | bytes 2097152 | tf_op jit(solution)/shard_map/all_to_all | solution.py:974
  (96 other events, 790.8 us)
where the time goes:
time: 346 us; the launch traced here: 340 us
  starting transfers between devices  126 us (36%)
  Pallas kernels  120 us (35%)
  waiting for transfers between devices  55.4 us (16%)
  local copies, waits for them, and re-layouts  33.3 us (10%)
  other arithmetic  4.22 us (1%)
    pallas_call x27, Pallas kernels, call(): pl.pallas_call(kernel, out_shape=outs, in_specs=[SMEM] * smem + [HBM] * h...  120 us
    ppermute x31, waiting for transfers between devices, shift(): lax.ppermute(value, 'narrow', [(i, (i + 2 * step) % 8) for i in range(8)])  46.6 us
    ppermute x31, starting transfers between devices, shift(): lax.ppermute(value, 'narrow', [(i, (i + 2 * step) % 8) for i in range(8)])  39.4 us
    all_to_all x4, starting transfers between devices, exchange(): lax.all_to_all(value, ('wide', 'narrow'), 0, 0, tiled=True, axis_index_gr...  38.6 us
    unnamed x133, local copies, waits for them, and re-layouts  30.5 us
    ppermute x10, starting transfers between devices, flip(): return lax.ppermute(value, axis, [(i, i ^ mask) for i in range(size)])  12.5 us
    ppermute x14, starting transfers between devices, swap(): return lax.ppermute(value, 'narrow', [(i, i ^ 1) for i in range(8)])  11.9 us
    ppermute x10, waiting for transfers between devices, flip(): return lax.ppermute(value, axis, [(i, i ^ mask) for i in range(size)])  7.56 us
  transfers between devices with their start and end apart: 63, of which 16 were waited for; matrix products, arithmetic and copies ran while one was open for 2% of the time, Pallas kernels for 34%

commit v1 on v0

--- a/solution.py
+++ b/solution.py
@@ -58,7 +58,7 @@
 
 
 MEBIBYTES = {
-    "attend_forward": 30,
+    "attend_forward": 56,
     "attend_backward": 56,
     "dispatch": 56,
     "halves": 56,
@@ -738,11 +738,14 @@
         size = lax.axis_size(axis)
         return lax.ppermute(value, axis, [(i, i ^ mask) for i in range(size)])
 
+    def sum_pairs(parts):
+        parts = [p.astype(F32) for p in parts]
+        return (parts[0] + parts[1]) + (parts[2] + parts[3])
+
     def sum_four(value, axis, unit):
         low = barrier(value.astype(BF16))
         parts = [low] + [flip(low, axis, mask * unit) for mask in (1, 2, 3)]
-        parts = [p.astype(F32) for p in parts]
-        return (parts[0] + parts[1]) + (parts[2] + parts[3])
+        return sum_pairs(parts)
 
     exchange_groups = [
         [w * 8 + chip * 2 + c for w in range(16) for c in range(2)] for chip in range(4)
@@ -948,28 +951,31 @@
     arrived_grads = lax.all_to_all(weight_grads.reshape(16, 32, WIDTH), "wide", 0, 0, tiled=True)
     gain_grad, sent, _ = barrier((gain_grad, sent, weight_grads))
 
-    small = sum_four(jnp.concatenate([router_terms, gain_grad, moe_gain_grad]), "narrow", 2)
-    got, small, returned = barrier((swap(sent), small, returned))
+    low = barrier(jnp.concatenate([router_terms, gain_grad, moe_gain_grad]).astype(BF16))
+    parts = [low] + [flip(low, "narrow", 2 * mask) for mask in (1, 2, 3)]
     kept = call(
         kept_kernel,
         "kept",
         [shape((TOK, WIDTH), BF16)] * 4,
-        [kept, got],
-    )
+        [kept, swap(sent)],
+    )
+    parts, kept = barrier((parts, kept))
+    small = sum_pairs(parts)
+    low = barrier(small.astype(BF16))
+    small = low.astype(F32) + flip(low, "narrow", 1).astype(F32)
+    small = jnp.concatenate(
+        [small, jnp.pad(bias_grad.reshape(1, 64), ((0, 0), (0, WIDTH - 64)))]
+    )
+    arrived_grads, kept = barrier((arrived_grads, kept))
+    copies = call(
+        share_kernel, "share", [shape((16, 32, WIDTH), BF16)], [arrived_grads]
+    )[0]
+    returned, _ = barrier((returned, copies))
     layer_out = call(
         combine_kernel,
         "combine",
         [shape((TOK, WIDTH), BF16)],
         [returned, middle, gates, token_picks],
-    )[0]
-    low = barrier(small.astype(BF16))
-    small = low.astype(F32) + flip(low, "narrow", 1).astype(F32)
-    small = jnp.concatenate(
-        [small, jnp.pad(bias_grad.reshape(1, 64), ((0, 0), (0, WIDTH - 64)))]
-    )
-    arrived_grads, kept, layer_out = barrier((arrived_grads, kept, layer_out))
-    copies = call(
-        share_kernel, "share", [shape((16, 32, WIDTH), BF16)], [arrived_grads]
     )[0]
     gathered = lax.all_to_all(copies, "wide", 0, 0, tiled=True).reshape(512, WIDTH)
     small = sum_four(small, "wide", 1)

time: 346 us -> 341 us (0.986)
  waiting for transfers between devices: 55.4 us -> 49.2 us
    ppermute x31, waiting for transfers between devices: 46.6 us -> 41.6 us  [shift(): lax.ppermute(value, 'narrow', [(i, (i + 2 * step) % 8) for i in range(8)])]
    unnamed x133 -> x141, local copies, waits for them, and re-layouts: 30.5 us -> 28.9 us
  transfers between devices with their start and end apart: 63 -> 63, of which waited for: 16 -> 15; matrix products, arithmetic and copies ran while one was open for 2% -> 2% of each run, Pallas kernels for 34% -> 35%
where the time goes in v1:
time: 341 us; the launch traced here: 335 us
  starting transfers between devices  126 us (37%)
  Pallas kernels  122 us (36%)
  waiting for transfers between devices  49.2 us (14%)
  local copies, waits for them, and re-layouts  32.9 us (10%)
    pallas_call x27, Pallas kernels, call(): pl.pallas_call(kernel, out_shape=outs, in_specs=[SMEM] * smem + [HBM] * h...  122 us
    ppermute x31, waiting for transfers between devices, shift(): lax.ppermute(value, 'narrow', [(i, (i + 2 * step) % 8) for i in range(8)])  41.6 us
    ppermute x31, starting transfers between devices, shift(): lax.ppermute(value, 'narrow', [(i, (i + 2 * step) % 8) for i in range(8)])  39.6 us
    all_to_all x4, starting transfers between devices, exchange(): lax.all_to_all(value, ('wide', 'narrow'), 0, 0, tiled=True, axis_index_gr...  38.6 us
    unnamed x141, local copies, waits for them, and re-layouts  28.9 us
    ppermute x10, starting transfers between devices, flip(): return lax.ppermute(value, axis, [(i, i ^ mask) for i in range(size)])  12.6 us
    ppermute x14, starting transfers between devices, swap(): return lax.ppermute(value, 'narrow', [(i, i ^ 1) for i in range(8)])  12.1 us
    all_to_all x1, starting transfers between devices, on_device(): lax.all_to_all(copies, 'wide', 0, 0, tiled=True).reshape(512, WIDTH)  6.91 us
  transfers between devices with their start and end apart: 63, of which 15 were waited for; matrix products, arithmetic and copies ran while one was open for 2% of the time, Pallas kernels for 35%

profile of v1, /device:TPU:1, one launch (start us, length us, event | category | flops | bytes accessed | tf_op | source)
XLA Modules:
  0.0 335.3 jit_solution(9574778326027586623)
XLA Ops:
  11.2 9.7 %all-to-all-start = ((bf16[32,16,1024]{2,1,0:T(8,128)(2,1)}), bf16[32,16,1024]{2,1,0:T(8,128)(2,1)S(1)}, u32[]{:S(2)}, u32[]{:S(2)}) async-start(bf16[32,16,1024]{2,1,0:T(8,128)(2,1)} %bitcast.10), calls=%async_computation | async-start | bytes 2097152 | tf_op jit(solution)/shard_map/all_to_all | solution.py:755
  28.1 13.1 %attend_forward.1 = (bf16[1408,1024]{1,0:T(8,128)(2,1)}, bf16[1408,512]{1,0:T(8,128)(2,1)}, bf16[1408,128]{1,0:T(8,128)(2,1)}, bf16[384,1024]{1,0:T(8,128)(2,1)}) custom-call(s32[8]{0:T(128)} %stack.44.place_ref.order_ref, f32[2,32]{1,0:T(2,128)} %convert_convert_fusion.bias_ref, bf16[176,1024]{1,0:T(8,128)(2,1)} %tok_ref.1, bf16[176,1024]{1,0:T(8,128)(2,1)} %copy-done.66, ...), custom_call_target="tpu_custom_call" | custom-call | flops 4600000000 | tf_op jit(solution)/shard_map/attend_forward/pallas_call | solution.py:75
  41.3 5.3 %all-to-all-start.1 = ((bf16[8,176,128]{2,1,0:T(8,128)(2,1)}), bf16[8,176,128]{2,1,0:T(8,128)(2,1)S(1)}, u32[]{:S(2)}, u32[]{:S(2)}) async-start(bf16[8,176,128]{2,1,0:T(8,128)(2,1)} %bitcast.48), calls=%async_computation.1 | async-start | bytes 720896 | tf_op jit(solution)/shard_map/all_to_all | solution.py:796
  47.6 6.1 %halves.1 = (bf16[768,1024]{1,0:T(8,128)(2,1)}, bf16[384,1024]{1,0:T(8,128)(2,1)}, bf16[768,1024]{1,0:T(8,128)(2,1)}, bf16[384,1024]{1,0:T(8,128)(2,1)}) custom-call(s32[2]{0:T(128)} %pad_add_fusion.core_ref, f32[2,2,352,1024]{3,2,1,0:T(8,128)} %bitcast.54, f32[2,352,1024]{2,1,0:T(8,128)} %down_ref), custom_call_target="tpu_custom_call" | custom-call | flops 57500000256 | tf_op jit(solution)/shard_map/halves/pallas_call | solution.py:75
  59.1 5.6 %dispatch.1 = (f32[176,1024]{1,0:T(8,128)}, f32[176,2]{1,0:T(8,128)}, bf16[512,1024]{1,0:T(8,128)(2,1)}, bf16[1024,1024]{1,0:T(8,128)(2,1)}) custom-call(s32[8]{0:T(128)} %stack.44.place_ref.order_ref, bf16[8,176,128]{2,1,0:T(8,128)(2,1)} %copy-done.3, bf16[128,1024]{1,0:T(8,128)(2,1)} %copy-done.56, bf16[128,1024]{1,0:T(8,128)(2,1)} %collective-permute-done.7.refs_1_, ...), custom_call_target="tpu_custom_call" | custom-call | flops 57500000256 | tf_op jit(solution)/shard_map/dispatch/pallas_call | solution.py:75
  64.6 9.5 %all-to-all-start.2 = ((bf16[32,16,1024]{2,1,0:T(8,128)(2,1)}), bf16[32,16,1024]{2,1,0:T(8,128)(2,1)S(1)}, u32[]{:S(2)}, u32[]{:S(2)}) async-start(bf16[32,16,1024]{2,1,0:T(8,128)(2,1)} %bitcast.47), calls=%async_computation.2 | async-start | bytes 2097152 | tf_op jit(solution)/shard_map/all_to_all | solution.py:755
  76.0 19.5 %collective-permute-done.16.refs_2_.refs_3_ = bf16[416,1024]{1,0:T(8,128)(2,1)} collective-permute-done((bf16[416,1024]{1,0:T(8,128)(2,1)S(1)}, bf16[416,1024]{1,0:T(8,128)(2,1)}, u32[]{:S(2)}, u32[]{:S(2)}) %collective-permute-start.16) | collective-permute-done | bytes 852000 | tf_op jit(solution)/shard_map/ppermute | solution.py:732
  101.3 6.6 %expert.3 = (bf16[416,768]{1,0:T(8,128)(2,1)S(1)}, bf16[416,1536]{1,0:T(8,128)(2,1)S(1)}, bf16[208,1024]{1,0:T(8,128)(2,1)S(1)}, bf16[208,1024]{1,0:T(8,128)(2,1...) custom-call(bf16[432,1024]{1,0:T(8,128)(2,1)S(1)} %unpack.3.refs_0_, ...), custom_call_target="tpu_custom_call" | custom-call | flops 57500000256 | tf_op jit(solution)/shard_map/expert/pallas_call | solution.py:75
  108.8 9.8 %collective-permute-done.17.refs_0_.refs_1_ = bf16[432,1024]{1,0:T(8,128)(2,1)S(1)} collective-permute-done((bf16[432,1024]{1,0:T(8,128)(2,1)S(1)}, bf16[432,1024]{1,0:T(8,128)(2,1)S(1)}, u32[]{:S(2)}, u32[]{:S(2)}) %collective-permute-start.17) | collective-permute-done | bytes 884768 | tf_op jit(solution)/shard_map/ppermute | solution.py:732
  118.8 3.1 collective-permute-start.22
  121.9 12.1 %expert.4 = (bf16[416,768]{1,0:T(8,128)(2,1)S(1)}, bf16[416,1536]{1,0:T(8,128)(2,1)S(1)}, bf16[208,1024]{1,0:T(8,128)(2,1)S(1)}, bf16[208,1024]{1,0:T(8,128)(2,1...) custom-call(bf16[432,1024]{1,0:T(8,128)(2,1)S(1)} %collective-permut, ...), custom_call_target="tpu_custom_call" | custom-call | flops 57500000256 | tf_op jit(solution)/shard_map/expert/pallas_call | solution.py:75
  136.9 2.8 collective-permute-start.26
  139.7 7.7 %expert.5 = (bf16[416,768]{1,0:T(8,128)(2,1)S(1)}, bf16[416,1536]{1,0:T(8,128)(2,1)S(1)}, bf16[208,1024]{1,0:T(8,128)(2,1)}, bf16[208,1024]{1,0:T(8,128)(2,1)}, ...) custom-call(bf16[208,1024]{1,0:T(8,128)(2,1)S(1)} %collective-permute-done.21.refs_0_.refs_3_, ...), custom_call_target="tpu_custom_call" | custom-call | flops 57500000256 | tf_op jit(solution)/shard_map/expert/pallas_call | solution.py:75
  147.4 2.7 collective-permute-start.23
  150.1 7.7 %pair_grad.1 = (f32[2,352,1024]{2,1,0:T(8,128)S(1)}, bf16[2,352,1024]{2,1,0:T(8,128)(2,1)S(1)}, f32[1664,128]{1,0:T(8,128)S(1)}) custom-call(bf16[432,1024]{1,0:T(8,128)(2,1)S(1)} %unpack.3.refs_0_, bf16[432,1024]{1,0:T(8,128)(2,1)S(1)} %collective-permute-done.17.refs_0_.refs_1_, bf16[432,1024]{1,0:T(8,128)(2,1)S(1)} %collective-permute-done.18.refs_2_, ...), custom_call_target="tpu_custom_call" | custom-call | flops 3449999872 | tf_op jit(solution)/shard_map/pair_grad/pallas_call | solution.py:75
  159.4 3.9 %collective-permute-start.29 = (bf16[2,352,1024]{2,1,0:T(8,128)(2,1)S(1)}, bf16[2,352,1024]{2,1,0:T(8,128)(2,1)S(1)}, u32[]{:S(2)}, u32[]{:S(2)}) collective-permute-start(bf16[2,352,1024]{2,1,0:T(8,128)(2,1)S(1)} %get-tuple-element.348), channel_id=1, source_target_pairs={{0,1},{1,0},{2,3},{3,2},{4,5},{5,4},{6,7},{7,6},{8,9},{9,8},{10,11... | collective-permute-start | bytes 4325384 | tf_op jit(solution)/shard_map/ppermute | solution.py:735
  167.9 5.1 %assemble_pair.1 = f32[2,2,352,1024]{3,2,1,0:T(8,128)} custom-call(s32[1]{0:T(128)} %bitcast.13.core_ref, f32[2,352,1024]{2,1,0:T(8,128)} %copy-done.5, bf16[2,352,1024]{2,1,0:T(8,128)(2,1)} %copy-done.54), custom_call_target="tpu_custom_call" | custom-call | flops 115000000 | tf_op jit(solution)/shard_map/assemble_pair/pallas_call | solution.py:75
  178.8 2.7 collective-permute-start.33
  183.5 10.5 %all-to-all-start.3 = ((bf16[32,16,1024]{2,1,0:T(8,128)(2,1)}), bf16[32,16,1024]{2,1,0:T(8,128)(2,1)}, u32[]{:S(2)}, u32[]{:S(2)}) async-start(bf16[32,16,1024]{2,1,0:T(8,128)(2,1)} %bitcast.20), calls=%async_computation.3 | async-start | bytes 2097152 | tf_op jit(solution)/shard_map/all_to_all | solution.py:755
  194.0 5.0 %collective-permute-done.32.near_top = bf16[208,1024]{1,0:T(8,128)(2,1)S(1)} collective-permute-done((bf16[208,1024]{1,0:T(8,128)(2,1)}, bf16[208,1024]{1,0:T(8,128)(2,1)S(1)}, u32[]{:S(2)}, u32[]{:S(2)}) %collective-permute-start.32) | collective-permute-done | bytes 426016 | tf_op jit(solution)/shard_map/ppermute | solution.py:732
  203.5 7.4 %down_grad.1 = (f32[1,352,1024]{2,1,0:T(8,128)}, bf16[1,352,1024]{2,1,0:T(8,128)(2,1)}) custom-call(bf16[416,1024]{1,0:T(8,128)(2,1)} %copy-done.17, bf16[416,1024]{1,0:T(8,128)(2,1)} %copy-done.37, bf16[416,1024]{1,0:T(8,128)(2,1)} %collective-permute-done.15.refs_3_.refs_2_, bf16[416,1024]{1,0:T(8,128)(2,1)} %collective-permute-done.16.refs_2_.refs_3_, ...), custom_call_target="tpu_custom_call" | custom-call | flops 57500000256 | tf_op jit(solution)/shard_map/down_grad/pallas_call | solution.py:75
  211.2 6.0 %middle_grad.1 = (f32[176,1024]{1,0:T(8,128)}, bf16[176,1024]{1,0:T(8,128)(2,1)}, bf16[8,176,128]{2,1,0:T(8,128)(2,1)}, f32[1,1024]{1,0:T(1,128)}, f32[176,32]{1,0:T(8,128)}) custom-call(bf16[512,1024]{1,0:T(8,128)(2,1)} %bitcast.21.rows_ref, f32[176,2]{1,0:T(8,128)} %get-tuple-element.368.gates_ref, f32[176,1024]{1,0:T(8,128)} %get-tuple-element.369.middle_ref, ...), custom_call_target="tpu_custom_call" | custom-call | flops 115000000 | tf_op jit(solution)/shard_map/middle_grad/pallas_call | solution.py:75
  220.0 2.9 collective-permute-start.36
  223.0 4.2 %all-to-all-start.4 = ((bf16[8,176,128]{2,1,0:T(8,128)(2,1)}), bf16[8,176,128]{2,1,0:T(8,128)(2,1)}, u32[]{:S(2)}, u32[]{:S(2)}) async-start(bf16[8,176,128]{2,1,0:T(8,128)(2,1)} %get-tuple-element.386), calls=%async_computation.4 | async-start | bytes 720896 | tf_op jit(solution)/shard_map/all_to_all | solution.py:918
  238.4 8.9 %all-to-all-start.5 = ((bf16[32,16,1024]{2,1,0:T(8,128)(2,1)}), bf16[32,16,1024]{2,1,0:T(8,128)(2,1)S(1)}, u32[]{:S(2)}, u32[]{:S(2)}) async-start(bf16[32,16,1024]{2,1,0:T(8,128)(2,1)} %bitcast.23), calls=%async_computation.5 | async-start | bytes 2097152 | tf_op jit(solution)/shard_map/all_to_all | solution.py:755
  250.4 21.9 %attend_backward.1 = (f32[2,32]{1,0:T(2,128)}, bf16[512,1024]{1,0:T(8,128)(2,1)}, f32[1,1024]{1,0:T(1,128)}, bf16[4,176,1024]{2,1,0:T(8,128)(2,1)}, bf16[4,176,1024]{2,1,0:T(8,128)(2,1)}) custom-call(s32[8]{0:T(128)} %stack.44.place_ref.order_ref, f32[2,32]{1,0:T(2,128)} %convert_convert_fusion.bias_ref, bf16[1408,1024]{1,0:T(8,128)(2,1)} %get-tuple-element.239.normed_hbm, ...), custom_call_target="tpu_custom_call" | custom-call | flops 57500000256 | tf_op jit(solution)/shard_map/attend_backward/pallas_call | solution.py:75
  275.7 6.9 %all-to-all-start.6 = ((bf16[16,32,1024]{2,1,0:T(8,128)(2,1)}), bf16[16,32,1024]{2,1,0:T(8,128)(2,1)}, u32[]{:S(2)}, u32[]{:S(2)}) async-start(bf16[16,32,1024]{2,1,0:T(8,128)(2,1)} %bitcast.34), calls=%async_computation.6 | async-start | bytes 2097152 | tf_op jit(solution)/shard_map/all_to_all | solution.py:951
  294.3 2.8 collective-permute-start.47
  305.3 6.9 %all-to-all-start.7 = ((bf16[16,32,1024]{2,1,0:T(8,128)(2,1)}), bf16[16,32,1024]{2,1,0:T(8,128)(2,1)S(1)}, u32[]{:S(2)}, u32[]{:S(2)}) async-start(bf16[16,32,1024]{2,1,0:T(8,128)(2,1)} %copy-done.12), calls=%async_computation.7 | async-start | bytes 2097152 | tf_op jit(solution)/shard_map/all_to_all | solution.py:980
  317.2 3.4 %collective-permute-start.53 = (bf16[35,1024]{1,0:T(8,128)(2,1)S(1)}, bf16[35,1024]{1,0:T(8,128)(2,1)S(1)}, u32[]{:S(2)}, u32[]{:S(2)}) collective-permute-start(bf16[35,1024]{1,0:T(8,128)(2,1)S(1)} %add_add_fusion.1), channel_id=1, source_target_pairs={{0,96},{8,104},{16,112},{24,120},{32,64},{40,72},{48,80},{56,88},{... | collective-permute-start | bytes 215048 | tf_op jit(solution)/shard_map/ppermute | solution.py:739
  321.2 3.3 assemble_down.1
  327.0 4.5 %collective-permute-done.53 = bf16[35,1024]{1,0:T(8,128)(2,1)S(1)} collective-permute-done((bf16[35,1024]{1,0:T(8,128)(2,1)S(1)}, bf16[35,1024]{1,0:T(8,128)(2,1)S(1)}, u32[]{:S(2)}, u32[]{:S(2)}) %collective-permute-start.53) | collective-permute-done | bytes 71712 | tf_op jit(solution)/shard_map/ppermute | solution.py:739
  (288 shorter events, 106.0 us)
Async XLA Ops:
  0.6 20.6 %collective-permute-start = (bf16[176,1024]{1,0:T(8,128)(2,1)}, bf16[176,1024]{1,0:T(8,128)(2,1)S(1)}, u32[]{:S(2)}, u32[]{:S(2)}) collective-permute-start(bf16[176,1024]{1,0:T(8,128)(2,1)} %tok_ref.1), channel_id=1, source_target_pairs={{0,2},{1,3},{2,4},{3,5},{4,6},{5,7},{6,0},{7,1},{8,10},{9,11},{10,... | collective-permute-start | bytes 1081352 | tf_op jit(solution)/shard_map/ppermute | solution.py:732
  2.8 18.8 %collective-permute-start.1 = (bf16[176,1024]{1,0:T(8,128)(2,1)}, bf16[176,1024]{1,0:T(8,128)(2,1)S(1)}, u32[]{:S(2)}, u32[]{:S(2)}) collective-permute-start(bf16[176,1024]{1,0:T(8,128)(2,1)} %tok_ref.1), channel_id=1, source_target_pairs={{0,6},{1,7},{2,0},{3,1},{4,2},{5,3},{6,4},{7,5},{8,14},{9,15},{10,... | collective-permute-start | bytes 1081352 | tf_op jit(solution)/shard_map/ppermute | solution.py:732
  4.1 17.7 %collective-permute-start.2 = (bf16[176,1024]{1,0:T(8,128)(2,1)}, bf16[176,1024]{1,0:T(8,128)(2,1)}, u32[]{:S(2)}, u32[]{:S(2)}) collective-permute-start(bf16[176,1024]{1,0:T(8,128)(2,1)} %tok_ref.1), channel_id=1, source_target_pairs={{0,4},{1,5},{2,6},{3,7},{4,0},{5,1},{6,2},{7,3},{8,12},{9,13},{10,... | collective-permute-start | bytes 1081352 | tf_op jit(solution)/shard_map/ppermute | solution.py:732
  11.2 30.1 %all-to-all-start = ((bf16[32,16,1024]{2,1,0:T(8,128)(2,1)}), bf16[32,16,1024]{2,1,0:T(8,128)(2,1)S(1)}, u32[]{:S(2)}, u32[]{:S(2)}) async-start(bf16[32,16,1024]{2,1,0:T(8,128)(2,1)} %bitcast.10), calls=%async_computation | async-start | bytes 2097152 | tf_op jit(solution)/shard_map/all_to_all | solution.py:755
  25.2 16.1 %collective-permute-start.7 = (bf16[128,1024]{1,0:T(8,128)(2,1)S(1)}, bf16[128,1024]{1,0:T(8,128)(2,1)}, u32[]{:S(2)}, u32[]{:S(2)}) collective-permute-start(bf16[128,1024]{1,0:T(8,128)(2,1)S(1)} %convert_element_type.63.refs_0_), channel_id=1, source_target_pairs={{0,2},{1,3},{2,4},{3,5},{4,6},{5,7},{6,0},{7,1},{8,10},{9,11},{10,... | collective-permute-start | bytes 786440 | tf_op jit(solution)/shard_map/ppermute | solution.py:732
  26.1 15.2 %collective-permute-start.8 = (bf16[128,1024]{1,0:T(8,128)(2,1)S(1)}, bf16[128,1024]{1,0:T(8,128)(2,1)}, u32[]{:S(2)}, u32[]{:S(2)}) collective-permute-start(bf16[128,1024]{1,0:T(8,128)(2,1)S(1)} %convert_element_type.63.refs_0_), channel_id=1, source_target_pairs={{0,6},{1,7},{2,0},{3,1},{4,2},{5,3},{6,4},{7,5},{8,14},{9,15},{10,... | collective-permute-start | bytes 786440 | tf_op jit(solution)/shard_map/ppermute | solution.py:732
  54.4 21.3 %collective-permute-start.14 = (bf16[416,1024]{1,0:T(8,128)(2,1)S(1)}, bf16[416,1024]{1,0:T(8,128)(2,1)S(1)}, u32[]{:S(2)}, u32[]{:S(2)}) collective-permute-start(bf16[416,1024]{1,0:T(8,128)(2,1)S(1)} %unpack.2.refs_1_.refs_0_), channel_id=1, source_target_pairs={{0,2},{1,3},{2,4},{3,5},{4,6},{5,7},{6,0},{7,1},{8,10},{9,11},{10,... | collective-permute-start | bytes 2555912 | tf_op jit(solution)/shard_map/ppermute | solution.py:732
  56.1 20.0 %collective-permute-start.15 = (bf16[416,1024]{1,0:T(8,128)(2,1)S(1)}, bf16[416,1024]{1,0:T(8,128)(2,1)}, u32[]{:S(2)}, u32[]{:S(2)}) collective-permute-start(bf16[416,1024]{1,0:T(8,128)(2,1)S(1)} %unpack.2.refs_1_.refs_0_), channel_id=1, source_target_pairs={{0,6},{1,7},{2,0},{3,1},{4,2},{5,3},{6,4},{7,5},{8,14},{9,15},{10,... | collective-permute-start | bytes 2555912 | tf_op jit(solution)/shard_map/ppermute | solution.py:732
  57.4 38.2 %collective-permute-start.16 = (bf16[416,1024]{1,0:T(8,128)(2,1)S(1)}, bf16[416,1024]{1,0:T(8,128)(2,1)}, u32[]{:S(2)}, u32[]{:S(2)}) collective-permute-start(bf16[416,1024]{1,0:T(8,128)(2,1)S(1)} %unpack.2.refs_1_.refs_0_), channel_id=1, source_target_pairs={{0,4},{1,5},{2,6},{3,7},{4,0},{5,1},{6,2},{7,3},{8,12},{9,13},{10,... | collective-permute-start | bytes 2555912 | tf_op jit(solution)/shard_map/ppermute | solution.py:732
  64.6 31.8 %all-to-all-start.2 = ((bf16[32,16,1024]{2,1,0:T(8,128)(2,1)}), bf16[32,16,1024]{2,1,0:T(8,128)(2,1)S(1)}, u32[]{:S(2)}, u32[]{:S(2)}) async-start(bf16[32,16,1024]{2,1,0:T(8,128)(2,1)} %bitcast.47), calls=%async_computation.2 | async-start | bytes 2097152 | tf_op jit(solution)/shard_map/all_to_all | solution.py:755
  74.1 26.0 %collective-permute-start.19 = (bf16[768,1024]{1,0:T(8,128)(2,1)}, bf16[768,1024]{1,0:T(8,128)(2,1)}, u32[]{:S(2)}, u32[]{:S(2)}) collective-permute-start(bf16[768,1024]{1,0:T(8,128)(2,1)} %get-tuple-element.268), channel_id=1, source_target_pairs={{0,1},{1,0},{2,3},{3,2},{4,5},{5,4},{6,7},{7,6},{8,9},{9,8},{10,11... | collective-permute-start | bytes 4718600 | tf_op jit(solution)/shard_map/ppermute | solution.py:735
  74.4 25.7 %collective-permute-start.20 = (bf16[384,1024]{1,0:T(8,128)(2,1)}, bf16[384,1024]{1,0:T(8,128)(2,1)}, u32[]{:S(2)}, u32[]{:S(2)}) collective-permute-start(bf16[384,1024]{1,0:T(8,128)(2,1)} %get-tuple-element.270), channel_id=1, source_target_pairs={{0,1},{1,0},{2,3},{3,2},{4,5},{5,4},{6,7},{7,6},{8,9},{9,8},{10,11... | collective-permute-start | bytes 2359304 | tf_op jit(solution)/shard_map/ppermute | solution.py:735
  97.4 21.2 %collective-permute-start.17 = (bf16[432,1024]{1,0:T(8,128)(2,1)S(1)}, bf16[432,1024]{1,0:T(8,128)(2,1)S(1)}, u32[]{:S(2)}, u32[]{:S(2)}) collective-permute-start(bf16[432,1024]{1,0:T(8,128)(2,1)S(1)} %unpack.3.refs_0_), channel_id=1, source_target_pairs={{0,2},{1,3},{2,4},{3,5},{4,6},{5,7},{6,0},{7,1},{8,10},{9,11},{10,... | collective-permute-start | bytes 2654216 | tf_op jit(solution)/shard_map/ppermute | solution.py:732
  98.0 20.6 %collective-permute-start.18 = (bf16[432,1024]{1,0:T(8,128)(2,1)S(1)}, bf16[432,1024]{1,0:T(8,128)(2,1)S(1)}, u32[]{:S(2)}, u32[]{:S(2)}) collective-permute-start(bf16[432,1024]{1,0:T(8,128)(2,1)S(1)} %unpack.3.refs_0_), channel_id=1, source_target_pairs={{0,6},{1,7},{2,0},{3,1},{4,2},{5,3},{6,4},{7,5},{8,14},{9,15},{10,... | collective-permute-start | bytes 2654216 | tf_op jit(solution)/shard_map/ppermute | solution.py:732
  118.6 18.2 %collective-permute-start.21 = (bf16[208,1024]{1,0:T(8,128)(2,1)S(1)}, bf16[208,1024]{1,0:T(8,128)(2,1)S(1)}, u32[]{:S(2)}, u32[]{:S(2)}) collective-permute-start(bf16[208,1024]{1,0:T(8,128)(2,1)S(1)} %slice.18), channel_id=1, source_target_pairs={{0,2},{1,3},{2,4},{3,5},{4,6},{5,7},{6,0},{7,1},{8,10},{9,11},{10,... | collective-permute-start | bytes 1277960 | tf_op jit(solution)/shard_map/ppermute | solution.py:732
  118.8 18.0 %collective-permute-start.22 = (bf16[224,1024]{1,0:T(8,128)(2,1)S(1)}, bf16[224,1024]{1,0:T(8,128)(2,1)S(1)}, u32[]{:S(2)}, u32[]{:S(2)}) collective-permute-start(bf16[224,1024]{1,0:T(8,128)(2,1)S(1)} %slice.19), channel_id=1, source_target_pairs={{0,6},{1,7},{2,0},{3,1},{4,2},{5,3},{6,4},{7,5},{8,14},{9,15},{10,... | collective-permute-start | bytes 1376264 | tf_op jit(solution)/shard_map/ppermute | solution.py:732
  177.1 16.9 %collective-permute-start.30 = (bf16[208,1024]{1,0:T(8,128)(2,1)}, bf16[208,1024]{1,0:T(8,128)(2,1)S(1)}, u32[]{:S(2)}, u32[]{:S(2)}) collective-permute-start(bf16[208,1024]{1,0:T(8,128)(2,1)} %get-tuple-element.357), channel_id=1, source_target_pairs={{0,6},{1,7},{2,0},{3,1},{4,2},{5,3},{6,4},{7,5},{8,14},{9,15},{10,... | collective-permute-start | bytes 1277960 | tf_op jit(solution)/shard_map/ppermute | solution.py:732
  178.8 15.3 %collective-permute-start.31 = (bf16[208,1024]{1,0:T(8,128)(2,1)}, bf16[208,1024]{1,0:T(8,128)(2,1)S(1)}, u32[]{:S(2)}, u32[]{:S(2)}) collective-permute-start(bf16[208,1024]{1,0:T(8,128)(2,1)} %get-tuple-element.358), channel_id=1, source_target_pairs={{0,2},{1,3},{2,4},{3,5},{4,6},{5,7},{6,0},{7,1},{8,10},{9,11},{10,... | collective-permute-start | bytes 1277960 | tf_op jit(solution)/shard_map/ppermute | solution.py:732
  178.8 20.2 %collective-permute-start.32 = (bf16[208,1024]{1,0:T(8,128)(2,1)}, bf16[208,1024]{1,0:T(8,128)(2,1)S(1)}, u32[]{:S(2)}, u32[]{:S(2)}) collective-permute-start(bf16[208,1024]{1,0:T(8,128)(2,1)} %get-tuple-element.359), channel_id=1, source_target_pairs={{0,2},{1,3},{2,4},{3,5},{4,6},{5,7},{6,0},{7,1},{8,10},{9,11},{10,... | collective-permute-start | bytes 1277960 | tf_op jit(solution)/shard_map/ppermute | solution.py:732
  178.8 20.2 %collective-permute-start.33 = (bf16[208,1024]{1,0:T(8,128)(2,1)}, bf16[208,1024]{1,0:T(8,128)(2,1)S(1)}, u32[]{:S(2)}, u32[]{:S(2)}) collective-permute-start(bf16[208,1024]{1,0:T(8,128)(2,1)} %get-tuple-element.360), channel_id=1, source_target_pairs={{0,6},{1,7},{2,0},{3,1},{4,2},{5,3},{6,4},{7,5},{8,14},{9,15},{10,... | collective-permute-start | bytes 1277960 | tf_op jit(solution)/shard_map/ppermute | solution.py:732
  183.5 27.7 %all-to-all-start.3 = ((bf16[32,16,1024]{2,1,0:T(8,128)(2,1)}), bf16[32,16,1024]{2,1,0:T(8,128)(2,1)}, u32[]{:S(2)}, u32[]{:S(2)}) async-start(bf16[32,16,1024]{2,1,0:T(8,128)(2,1)} %bitcast.20), calls=%async_computation.3 | async-start | bytes 2097152 | tf_op jit(solution)/shard_map/all_to_all | solution.py:755
  202.1 15.2 %collective-permute-start.34 = (bf16[208,1024]{1,0:T(8,128)(2,1)}, bf16[208,1024]{1,0:T(8,128)(2,1)S(1)}, u32[]{:S(2)}, u32[]{:S(2)}) collective-permute-start(bf16[208,1024]{1,0:T(8,128)(2,1)} %get-tuple-element.383), channel_id=1, source_target_pairs={{0,6},{1,7},{2,0},{3,1},{4,2},{5,3},{6,4},{7,5},{8,14},{9,15},{10,... | collective-permute-start | bytes 1277960 | tf_op jit(solution)/shard_map/ppermute | solution.py:732
  202.2 15.0 %collective-permute-start.35 = (bf16[208,1024]{1,0:T(8,128)(2,1)}, bf16[208,1024]{1,0:T(8,128)(2,1)S(1)}, u32[]{:S(2)}, u32[]{:S(2)}) collective-permute-start(bf16[208,1024]{1,0:T(8,128)(2,1)} %get-tuple-element.384), channel_id=1, source_target_pairs={{0,2},{1,3},{2,4},{3,5},{4,6},{5,7},{6,0},{7,1},{8,10},{9,11},{10,... | collective-permute-start | bytes 1277960 | tf_op jit(solution)/shard_map/ppermute | solution.py:732
  238.4 33.9 %all-to-all-start.5 = ((bf16[32,16,1024]{2,1,0:T(8,128)(2,1)}), bf16[32,16,1024]{2,1,0:T(8,128)(2,1)S(1)}, u32[]{:S(2)}, u32[]{:S(2)}) async-start(bf16[32,16,1024]{2,1,0:T(8,128)(2,1)} %bitcast.23), calls=%async_computation.5 | async-start | bytes 2097152 | tf_op jit(solution)/shard_map/all_to_all | solution.py:755
  247.3 24.9 %collective-permute-start.37 = (bf16[128,1024]{1,0:T(8,128)(2,1)}, bf16[128,1024]{1,0:T(8,128)(2,1)S(1)}, u32[]{:S(2)}, u32[]{:S(2)}) collective-permute-start(bf16[128,1024]{1,0:T(8,128)(2,1)} %get-tuple-element.405), channel_id=1, source_target_pairs={{0,6},{1,7},{2,0},{3,1},{4,2},{5,3},{6,4},{7,5},{8,14},{9,15},{10,... | collective-permute-start | bytes 786440 | tf_op jit(solution)/shard_map/ppermute | solution.py:732
  248.6 23.6 %collective-permute-start.38 = (bf16[128,1024]{1,0:T(8,128)(2,1)}, bf16[128,1024]{1,0:T(8,128)(2,1)S(1)}, u32[]{:S(2)}, u32[]{:S(2)}) collective-permute-start(bf16[128,1024]{1,0:T(8,128)(2,1)} %get-tuple-element.406), channel_id=1, source_target_pairs={{0,2},{1,3},{2,4},{3,5},{4,6},{5,7},{6,0},{7,1},{8,10},{9,11},{10,... | collective-permute-start | bytes 786440 | tf_op jit(solution)/shard_map/ppermute | solution.py:732
  248.9 23.4 %collective-permute-start.39 = (bf16[128,1024]{1,0:T(8,128)(2,1)}, bf16[128,1024]{1,0:T(8,128)(2,1)S(1)}, u32[]{:S(2)}, u32[]{:S(2)}) collective-permute-start(bf16[128,1024]{1,0:T(8,128)(2,1)} %copy-done.42), channel_id=1, source_target_pairs={{0,4},{1,5},{2,6},{3,7},{4,0},{5,1},{6,2},{7,3},{8,12},{9,13},{10,... | collective-permute-start | bytes 786440 | tf_op jit(solution)/shard_map/ppermute | solution.py:732
  275.7 23.6 %all-to-all-start.6 = ((bf16[16,32,1024]{2,1,0:T(8,128)(2,1)}), bf16[16,32,1024]{2,1,0:T(8,128)(2,1)}, u32[]{:S(2)}, u32[]{:S(2)}) async-start(bf16[16,32,1024]{2,1,0:T(8,128)(2,1)} %bitcast.34), calls=%async_computation.6 | async-start | bytes 2097152 | tf_op jit(solution)/shard_map/all_to_all | solution.py:951
  297.7 23.5 %collective-permute-start.54 = (bf16[1,352,1024]{2,1,0:T(8,128)(2,1)}, bf16[1,352,1024]{2,1,0:T(8,128)(2,1)}, u32[]{:S(2)}, u32[]{:S(2)}) collective-permute-start(bf16[1,352,1024]{2,1,0:T(8,128)(2,1)} %get-tuple-element.451), channel_id=1, source_target_pairs={{0,1},{1,0},{2,3},{3,2},{4,5},{5,4},{6,7},{7,6},{8,9},{9,8},{10,11... | collective-permute-start | bytes 2162696 | tf_op jit(solution)/shard_map/ppermute | solution.py:735
  299.4 16.0 %collective-permute-start.48 = (bf16[176,1024]{1,0:T(8,128)(2,1)}, bf16[176,1024]{1,0:T(8,128)(2,1)S(1)}, u32[]{:S(2)}, u32[]{:S(2)}) collective-permute-start(bf16[176,1024]{1,0:T(8,128)(2,1)} %copy-done.40), channel_id=1, source_target_pairs={{0,6},{1,7},{2,0},{3,1},{4,2},{5,3},{6,4},{7,5},{8,14},{9,15},{10,... | collective-permute-start | bytes 1081352 | tf_op jit(solution)/shard_map/ppermute | solution.py:732
  301.0 16.2 %collective-permute-start.50 = (bf16[176,1024]{1,0:T(8,128)(2,1)}, bf16[176,1024]{1,0:T(8,128)(2,1)}, u32[]{:S(2)}, u32[]{:S(2)}) collective-permute-start(bf16[176,1024]{1,0:T(8,128)(2,1)} %copy-done.38), channel_id=1, source_target_pairs={{0,4},{1,5},{2,6},{3,7},{4,0},{5,1},{6,2},{7,3},{8,12},{9,13},{10,... | collective-permute-start | bytes 1081352 | tf_op jit(solution)/shard_map/ppermute | solution.py:732
  305.3 28.2 %all-to-all-start.7 = ((bf16[16,32,1024]{2,1,0:T(8,128)(2,1)}), bf16[16,32,1024]{2,1,0:T(8,128)(2,1)S(1)}, u32[]{:S(2)}, u32[]{:S(2)}) async-start(bf16[16,32,1024]{2,1,0:T(8,128)(2,1)} %copy-done.12), calls=%async_computation.7 | async-start | bytes 2097152 | tf_op jit(solution)/shard_map/all_to_all | solution.py:980
  (100 other events, 760.0 us)

commit v2 on v1

--- a/solution.py
+++ b/solution.py
@@ -46,7 +46,6 @@
     "dispatch": 50,
     "slots": 50,
     "collect": 50,
-    "down_grad": 50,
     "halves": 50,
     "attend_forward": 4,
     "attend_backward": 50,
@@ -456,16 +455,23 @@
     )[0]
 
 
-def expert_kernel(counts, *refs):
+def expert_kernel(counts, merge, *refs):
     groups = []
     for count in counts:
         groups.append(refs[: count + 1])
         refs = refs[count + 1 :]
     pair_ref, pair_new_ref, down_ref, down_new_ref = refs[:4]
     refs = refs[4:]
+    if merge:
+        left_end, right_top = refs[:2]
+        refs = refs[2:]
     for *rows_refs, grads_ref in groups:
         mid_ref, inner_ref, out_top_ref, out_end_ref, back_top_ref, back_end_ref = refs[:6]
         refs = refs[6:]
+        if merge:
+            out_top_ref[HALF:, :] = left_end[...]
+            out_end_ref[:HALF, :] = right_top[...]
+            out_top_ref, out_end_ref = out_top_ref.at[:HALF], out_end_ref.at[HALF:]
         if len(rows_refs) == 1:
             rows = rows_refs[0][:ROWS, :]
         else:
@@ -503,20 +509,21 @@
         out_end_ref[...] = out[HALF:]
 
 
-def run_expert(chunks, weights):
+def run_expert(chunks, weights, merged=()):
+    sent = ROWS if merged else HALF
     results = call(
-        functools.partial(expert_kernel, [len(rows) for rows, _ in chunks]),
+        functools.partial(expert_kernel, [len(rows) for rows, _ in chunks], bool(merged)),
         "expert",
         [
             shape((ROWS, FULL), BF16),
             shape((ROWS, 2 * FULL), BF16),
-            shape((HALF, WIDTH), BF16),
-            shape((HALF, WIDTH), BF16),
+            shape((sent, WIDTH), BF16),
+            shape((sent, WIDTH), BF16),
             shape((HALF, WIDTH), BF16),
             shape((TILED - HALF, WIDTH), BF16),
         ]
         * len(chunks),
-        [a for rows, grads in chunks for a in (*rows, grads)] + weights,
+        [a for rows, grads in chunks for a in (*rows, grads)] + weights + list(merged),
     )
     return [list(results[6 * i : 6 * i + 6]) for i in range(len(chunks))]
 
@@ -846,7 +853,7 @@
     results += run_expert([([row_left], cot_parts[1]), ([row_right], cot_parts[2])], weights)
     over, results = barrier((over, results))
     row_parts = row_parts + over
-    results += run_expert([(over, cot_parts[3])], weights)
+    results += run_expert([(over, cot_parts[3])], weights, [results[1][3], results[2][2]])
     mids, inners = ([r[i] for r in results] for i in range(2))
     outs, backs = [r[2:4] for r in results], [r[4:6] for r in results]
 
@@ -887,11 +894,10 @@
         smem=1,
     )[0]
     pieces, outs, mids, pair_grads = barrier((arrive(landed), outs, mids, pair_grads))
-    out_far, out_near = leave_far(outs[3]), leave_near(*outs[1:3])
+    from_right, from_left = leave_far(outs[3])
     back = call(collect_kernel, "collect", [shape((EXPERTS * SLOTS, WIDTH), BF16)], pieces)[0]
     row_grads = blocks(back)
-    mids, out_far, out_near, _ = barrier((mids, out_far, out_near, back))
-    out_parts = arrive(land(*outs[:3], out_near, out_far))
+    mids, _ = barrier((mids, back))
     down_part, down_low = call(
         down_grad_kernel,
         "down_grad",
@@ -899,7 +905,11 @@
         [*cot_parts, *mids, gate_columns],
         [pltpu.VMEM((4 * ROWS, WIDTH), BF16)],
     )
-    row_grads, down_part = barrier((row_grads, down_part))
+    from_right, from_left, down_part = barrier((from_right, from_left, down_part))
+    out_near, out_far = [from_left[:HALF], from_right[HALF:]], [from_right[:HALF], from_left[HALF:]]
+    out_landed = land(*outs[:3], out_near, out_far)
+    row_grads, down_part, out_landed = barrier((row_grads, down_part, out_landed))
+    out_parts = arrive(out_landed)
     middle_grad, middle_low, send_heads, moe_gain_grad, logit_grads = call(
         middle_grad_kernel,
         "middle_grad",
@@ -916,7 +926,6 @@
         ],
     )
     head_grads = lax.all_to_all(send_heads, "narrow", 0, 0, tiled=True).reshape(LEN, 128)
-    middle_low, out_parts = barrier((middle_low, out_parts))
     outer_sent = call(
         outer_sent_kernel,
         "outer_sent",
@@ -925,7 +934,7 @@
         smem=1,
     )[0]
     back_out = call(collect_out_kernel, "collect_out", [shape((EXPERTS * SLOTS, WIDTH), BF16)], out_parts)[0]
-    outer_got, head_grads, back_out = barrier((swap(outer_sent), head_grads, back_out))
+    outer_got = swap(outer_sent)
     router_terms, *outer_parts = call(
         outer_kept_kernel,
         "outer_kept",

time: 341 us -> 341 us (level)
  waiting for transfers between devices: 49.2 us -> 56 us
  starting transfers between devices: 126 us -> 121 us
    all_to_all x4, waiting for transfers between devices: 0.33 us -> 4.68 us  [exchange(): lax.all_to_all(value, ('wide', 'narrow'), 0, 0, tiled=True, axis_index_gr...]
    ppermute x31 -> x29, waiting for transfers between devices: 41.6 us -> 45 us  [shift(): lax.ppermute(value, 'narrow', [(i, (i + 2 * step) % 8) for i in range(8)])]
    unnamed x141 -> x133, local copies, waits for them, and re-layouts: 28.9 us -> 25.8 us
    ppermute x31 -> x29, starting transfers between devices: 39.6 us -> 38.4 us  [shift(): lax.ppermute(value, 'narrow', [(i, (i + 2 * step) % 8) for i in range(8)])]
  transfers between devices with their start and end apart: 63 -> 61, of which waited for: 15 -> 15; matrix products, arithmetic and copies ran while one was open for 2% -> 3% of each run, Pallas kernels for 35% -> 34%
where the time goes in v2:
time: 341 us; the launch traced here: 335 us
  Pallas kernels  122 us (36%)
  starting transfers between devices  121 us (35%)
  waiting for transfers between devices  56 us (16%)
  local copies, waits for them, and re-layouts  31.3 us (9%)
    pallas_call x27, Pallas kernels, call(): pl.pallas_call(kernel, out_shape=outs, in_specs=[SMEM] * smem + [HBM] * h...  122 us
    ppermute x29, waiting for transfers between devices, shift(): lax.ppermute(value, 'narrow', [(i, (i + 2 * step) % 8) for i in range(8)])  45 us
    ppermute x29, starting transfers between devices, shift(): lax.ppermute(value, 'narrow', [(i, (i + 2 * step) % 8) for i in range(8)])  38.4 us
    all_to_all x4, starting transfers between devices, exchange(): lax.all_to_all(value, ('wide', 'narrow'), 0, 0, tiled=True, axis_index_gr...  36.1 us
    unnamed x133, local copies, waits for them, and re-layouts  25.8 us
    ppermute x10, starting transfers between devices, flip(): return lax.ppermute(value, axis, [(i, i ^ mask) for i in range(size)])  13 us
    ppermute x14, starting transfers between devices, swap(): return lax.ppermute(value, 'narrow', [(i, i ^ 1) for i in range(8)])  9.31 us
    all_to_all x1, starting transfers between devices, on_device(): lax.all_to_all(copies, 'wide', 0, 0, tiled=True).reshape(512, WIDTH)  7.09 us
  transfers between devices with their start and end apart: 61, of which 15 were waited for; matrix products, arithmetic and copies ran while one was open for 3% of the time, Pallas kernels for 34%

profile of v2, /device:TPU:1, one launch (start us, length us, event | category | flops | bytes accessed | tf_op | source)
XLA Modules:
  0.0 335.2 jit_solution(4572242642831871554)
XLA Ops:
  11.2 9.7 %all-to-all-start = ((bf16[32,16,1024]{2,1,0:T(8,128)(2,1)}), bf16[32,16,1024]{2,1,0:T(8,128)(2,1)S(1)}, u32[]{:S(2)}, u32[]{:S(2)}) async-start(bf16[32,16,1024]{2,1,0:T(8,128)(2,1)} %bitcast.10), calls=%async_computation | async-start | bytes 2097152 | tf_op jit(solution)/shard_map/all_to_all | solution.py:762
  28.1 13.1 %attend_forward.1 = (bf16[1408,1024]{1,0:T(8,128)(2,1)}, bf16[1408,512]{1,0:T(8,128)(2,1)}, bf16[1408,128]{1,0:T(8,128)(2,1)}, bf16[384,1024]{1,0:T(8,128)(2,1)}) custom-call(s32[8]{0:T(128)} %stack.44.place_ref.order_ref, f32[2,32]{1,0:T(2,128)} %convert_convert_fusion.bias_ref, bf16[176,1024]{1,0:T(8,128)(2,1)} %tok_ref.1, bf16[176,1024]{1,0:T(8,128)(2,1)} %copy-done.61, ...), custom_call_target="tpu_custom_call" | custom-call | flops 4600000000 | tf_op jit(solution)/shard_map/attend_forward/pallas_call | solution.py:74
  41.3 5.2 %all-to-all-start.1 = ((bf16[8,176,128]{2,1,0:T(8,128)(2,1)}), bf16[8,176,128]{2,1,0:T(8,128)(2,1)S(1)}, u32[]{:S(2)}, u32[]{:S(2)}) async-start(bf16[8,176,128]{2,1,0:T(8,128)(2,1)} %bitcast.48), calls=%async_computation.1 | async-start | bytes 720896 | tf_op jit(solution)/shard_map/all_to_all | solution.py:803
  47.6 6.1 %halves.1 = (bf16[768,1024]{1,0:T(8,128)(2,1)}, bf16[384,1024]{1,0:T(8,128)(2,1)}, bf16[768,1024]{1,0:T(8,128)(2,1)}, bf16[384,1024]{1,0:T(8,128)(2,1)}) custom-call(s32[2]{0:T(128)} %pad_add_fusion.core_ref, f32[2,2,352,1024]{3,2,1,0:T(8,128)} %bitcast.54, f32[2,352,1024]{2,1,0:T(8,128)} %down_ref), custom_call_target="tpu_custom_call" | custom-call | flops 57500000256 | tf_op jit(solution)/shard_map/halves/pallas_call | solution.py:74
  59.0 5.6 %dispatch.1 = (f32[176,1024]{1,0:T(8,128)}, f32[176,2]{1,0:T(8,128)}, bf16[512,1024]{1,0:T(8,128)(2,1)}, bf16[1024,1024]{1,0:T(8,128)(2,1)}) custom-call(s32[8]{0:T(128)} %stack.44.place_ref.order_ref, bf16[8,176,128]{2,1,0:T(8,128)(2,1)} %copy-done.4, bf16[128,1024]{1,0:T(8,128)(2,1)} %copy-done.51, bf16[128,1024]{1,0:T(8,128)(2,1)} %collective-permute-done.7.refs_1_, ...), custom_call_target="tpu_custom_call" | custom-call | flops 57500000256 | tf_op jit(solution)/shard_map/dispatch/pallas_call | solution.py:74
  64.6 9.4 %all-to-all-start.2 = ((bf16[32,16,1024]{2,1,0:T(8,128)(2,1)}), bf16[32,16,1024]{2,1,0:T(8,128)(2,1)S(1)}, u32[]{:S(2)}, u32[]{:S(2)}) async-start(bf16[32,16,1024]{2,1,0:T(8,128)(2,1)} %bitcast.47), calls=%async_computation.2 | async-start | bytes 2097152 | tf_op jit(solution)/shard_map/all_to_all | solution.py:762
  76.0 19.5 %collective-permute-done.16.refs_2_.refs_3_ = bf16[416,1024]{1,0:T(8,128)(2,1)} collective-permute-done((bf16[416,1024]{1,0:T(8,128)(2,1)S(1)}, bf16[416,1024]{1,0:T(8,128)(2,1)}, u32[]{:S(2)}, u32[]{:S(2)}) %collective-permute-start.16) | collective-permute-done | bytes 852000 | tf_op jit(solution)/shard_map/ppermute | solution.py:739
  101.2 6.6 %expert.3 = (bf16[416,768]{1,0:T(8,128)(2,1)S(1)}, bf16[416,1536]{1,0:T(8,128)(2,1)S(1)}, bf16[208,1024]{1,0:T(8,128)(2,1)S(1)}, bf16[208,1024]{1,0:T(8,128)(2,1...) custom-call(bf16[432,1024]{1,0:T(8,128)(2,1)S(1)} %unpack.3.refs_0_, ...), custom_call_target="tpu_custom_call" | custom-call | flops 57500000256 | tf_op jit(solution)/shard_map/expert/pallas_call | solution.py:74
  108.7 9.9 %collective-permute-done.17.refs_0_.refs_1_ = bf16[432,1024]{1,0:T(8,128)(2,1)S(1)} collective-permute-done((bf16[432,1024]{1,0:T(8,128)(2,1)S(1)}, bf16[432,1024]{1,0:T(8,128)(2,1)S(1)}, u32[]{:S(2)}, u32[]{:S(2)}) %collective-permute-start.17) | collective-permute-done | bytes 884768 | tf_op jit(solution)/shard_map/ppermute | solution.py:739
  118.7 3.1 collective-permute-start.22
  121.9 11.4 %expert.4 = (bf16[416,768]{1,0:T(8,128)(2,1)S(1)}, bf16[416,1536]{1,0:T(8,128)(2,1)S(1)}, bf16[208,1024]{1,0:T(8,128)(2,1)S(1)}, bf16[208,1024]{1,0:T(8,128)(2,1...) custom-call(bf16[432,1024]{1,0:T(8,128)(2,1)S(1)} %collective-permut, ...), custom_call_target="tpu_custom_call" | custom-call | flops 57500000256 | tf_op jit(solution)/shard_map/expert/pallas_call | solution.py:74
  140.0 6.9 %expert.5 = (bf16[416,768]{1,0:T(8,128)(2,1)S(1)}, bf16[416,1536]{1,0:T(8,128)(2,1)S(1)}, bf16[416,1024]{1,0:T(8,128)(2,1)S(1)}, bf16[416,1024]{1,0:T(8,128)(2,1...) custom-call(bf16[208,1024]{1,0:T(8,128)(2,1)S(1)} %collective-permute-done.21.refs_0_.refs_3_, ...), custom_call_target="tpu_custom_call" | custom-call | flops 57500000256 | tf_op jit(solution)/shard_map/expert/pallas_call | solution.py:74
  151.0 7.7 %pair_grad.1 = (f32[2,352,1024]{2,1,0:T(8,128)S(1)}, bf16[2,352,1024]{2,1,0:T(8,128)(2,1)S(1)}, f32[1664,128]{1,0:T(8,128)S(1)}) custom-call(bf16[432,1024]{1,0:T(8,128)(2,1)S(1)} %unpack.3.refs_0_, bf16[432,1024]{1,0:T(8,128)(2,1)S(1)} %collective-permute-done.17.refs_0_.refs_1_, bf16[432,1024]{1,0:T(8,128)(2,1)S(1)} %collective-permute-done.18.refs_2_, ...), custom_call_target="tpu_custom_call" | custom-call | flops 3449999872 | tf_op jit(solution)/shard_map/pair_grad/pallas_call | solution.py:74
  160.3 3.9 %collective-permute-start.29 = (bf16[2,352,1024]{2,1,0:T(8,128)(2,1)S(1)}, bf16[2,352,1024]{2,1,0:T(8,128)(2,1)}, u32[]{:S(2)}, u32[]{:S(2)}) collective-permute-start(bf16[2,352,1024]{2,1,0:T(8,128)(2,1)S(1)} %get-tuple-element.341), channel_id=1, source_target_pairs={{0,1},{1,0},{2,3},{3,2},{4,5},{5,4},{6,7},{7,6},{8,9},{9,8},{10,11... | collective-permute-start | bytes 4325384 | tf_op jit(solution)/shard_map/ppermute | solution.py:742
  167.7 5.1 %assemble_pair.1 = f32[2,2,352,1024]{3,2,1,0:T(8,128)} custom-call(s32[1]{0:T(128)} %bitcast.13.core_ref, f32[2,352,1024]{2,1,0:T(8,128)} %copy-done.6, bf16[2,352,1024]{2,1,0:T(8,128)(2,1)} %collective-permute-done.29.got_ref), custom_call_target="tpu_custom_call" | custom-call | flops 115000000 | tf_op jit(solution)/shard_map/assemble_pair/pallas_call | solution.py:74
  172.8 3.4 %collective-permute-done.27.got_top = bf16[208,1024]{1,0:T(8,128)(2,1)S(1)} collective-permute-done((bf16[208,1024]{1,0:T(8,128)(2,1)S(1)}, bf16[208,1024]{1,0:T(8,128)(2,1)S(1)}, u32[]{:S(2)}, u32[]{:S(2)}) %collective-permute-start.27) | collective-permute-done | bytes 426016 | tf_op jit(solution)/shard_map/ppermute | solution.py:739
  181.7 9.9 %all-to-all-start.3 = ((bf16[32,16,1024]{2,1,0:T(8,128)(2,1)}), bf16[32,16,1024]{2,1,0:T(8,128)(2,1)}, u32[]{:S(2)}, u32[]{:S(2)}) async-start(bf16[32,16,1024]{2,1,0:T(8,128)(2,1)} %bitcast.20), calls=%async_computation.3 | async-start | bytes 2097152 | tf_op jit(solution)/shard_map/all_to_all | solution.py:762
  191.6 7.4 %down_grad.1 = (f32[1,352,1024]{2,1,0:T(8,128)}, bf16[1,352,1024]{2,1,0:T(8,128)(2,1)}) custom-call(bf16[416,1024]{1,0:T(8,128)(2,1)} %copy-done.3, bf16[416,1024]{1,0:T(8,128)(2,1)} %copy-done.18, bf16[416,1024]{1,0:T(8,128)(2,1)} %collective-permute-done.15.refs_3_.refs_2_, bf16[416,1024]{1,0:T(8,128)(2,1)} %collective-permute-done.16.refs_2_.refs_3_, ...), custom_call_target="tpu_custom_call" | custom-call | flops 115000000 | tf_op jit(solution)/shard_map/down_grad/pallas_call | solution.py:74
  204.2 4.7 %all-to-all-done.3 = bf16[32,16,1024]{2,1,0:T(8,128)(2,1)} async-done(((bf16[32,16,1024]{2,1,0:T(8,128)(2,1)}), bf16[32,16,1024]{2,1,0:T(8,128)(2,1)}, u32[]{:S(2)}, u32[]{:S(2)}) %all-to-all-start.3) | async-done | bytes 1048608 | tf_op jit(solution)/shard_map/all_to_all | solution.py:762
  208.9 6.0 %middle_grad.1 = (f32[176,1024]{1,0:T(8,128)}, bf16[176,1024]{1,0:T(8,128)(2,1)}, bf16[8,176,128]{2,1,0:T(8,128)(2,1)}, f32[1,1024]{1,0:T(1,128)}, f32[176,32]{1,0:T(8,128)}) custom-call(bf16[512,1024]{1,0:T(8,128)(2,1)} %bitcast.21.rows_ref, f32[176,2]{1,0:T(8,128)} %get-tuple-element.370.gates_ref, f32[176,1024]{1,0:T(8,128)} %get-tuple-element.371.middle_ref, ...), custom_call_target="tpu_custom_call" | custom-call | flops 115000000 | tf_op jit(solution)/shard_map/middle_grad/pallas_call | solution.py:74
  217.3 3.0 collective-permute-start.32
  220.3 5.1 %all-to-all-start.4 = ((bf16[8,176,128]{2,1,0:T(8,128)(2,1)}), bf16[8,176,128]{2,1,0:T(8,128)(2,1)}, u32[]{:S(2)}, u32[]{:S(2)}) async-start(bf16[8,176,128]{2,1,0:T(8,128)(2,1)} %get-tuple-element.374), calls=%async_computation.4 | async-start | bytes 720896 | tf_op jit(solution)/shard_map/all_to_all | solution.py:928
  226.2 4.1 %collective-permute-done.32.got_top = bf16[208,1024]{1,0:T(8,128)(2,1)} collective-permute-done((bf16[208,1024]{1,0:T(8,128)(2,1)}, bf16[208,1024]{1,0:T(8,128)(2,1)}, u32[]{:S(2)}, u32[]{:S(2)}) %collective-permute-start.32) | collective-permute-done | bytes 426016 | tf_op jit(solution)/shard_map/ppermute | solution.py:739
  230.3 3.1 collective-permute-done.33.got_end
  235.7 2.9 collect_out.1
  240.4 7.0 %all-to-all-start.5 = ((bf16[32,16,1024]{2,1,0:T(8,128)(2,1)}), bf16[32,16,1024]{2,1,0:T(8,128)(2,1)S(1)}, u32[]{:S(2)}, u32[]{:S(2)}) async-start(bf16[32,16,1024]{2,1,0:T(8,128)(2,1)} %bitcast.23), calls=%async_computation.5 | async-start | bytes 2097152 | tf_op jit(solution)/shard_map/all_to_all | solution.py:762
  249.0 21.9 %attend_backward.1 = (f32[2,32]{1,0:T(2,128)}, bf16[512,1024]{1,0:T(8,128)(2,1)}, f32[1,1024]{1,0:T(1,128)}, bf16[4,176,1024]{2,1,0:T(8,128)(2,1)}, bf16[4,176,1024]{2,1,0:T(8,128)(2,1)}) custom-call(s32[8]{0:T(128)} %stack.44.place_ref.order_ref, f32[2,32]{1,0:T(2,128)} %convert_convert_fusion.bias_ref, bf16[1408,1024]{1,0:T(8,128)(2,1)} %get-tuple-element.232.normed_hbm, ...), custom_call_target="tpu_custom_call" | custom-call | flops 57500000256 | tf_op jit(solution)/shard_map/attend_backward/pallas_call | solution.py:74
  274.2 6.9 %all-to-all-start.6 = ((bf16[16,32,1024]{2,1,0:T(8,128)(2,1)}), bf16[16,32,1024]{2,1,0:T(8,128)(2,1)}, u32[]{:S(2)}, u32[]{:S(2)}) async-start(bf16[16,32,1024]{2,1,0:T(8,128)(2,1)} %bitcast.34), calls=%async_computation.6 | async-start | bytes 2097152 | tf_op jit(solution)/shard_map/all_to_all | solution.py:960
  305.1 7.1 %all-to-all-start.7 = ((bf16[16,32,1024]{2,1,0:T(8,128)(2,1)}), bf16[16,32,1024]{2,1,0:T(8,128)(2,1)S(1)}, u32[]{:S(2)}, u32[]{:S(2)}) async-start(bf16[16,32,1024]{2,1,0:T(8,128)(2,1)} %copy-done.13), calls=%async_computation.7 | async-start | bytes 2097152 | tf_op jit(solution)/shard_map/all_to_all | solution.py:989
  316.8 3.5 %collective-permute-start.51 = (bf16[35,1024]{1,0:T(8,128)(2,1)S(1)}, bf16[35,1024]{1,0:T(8,128)(2,1)S(1)}, u32[]{:S(2)}, u32[]{:S(2)}) collective-permute-start(bf16[35,1024]{1,0:T(8,128)(2,1)S(1)} %add_add_fusion.1), channel_id=1, source_target_pairs={{0,96},{8,104},{16,112},{24,120},{32,64},{40,72},{48,80},{56,88},{... | collective-permute-start | bytes 215048 | tf_op jit(solution)/shard_map/ppermute | solution.py:746
  320.9 3.3 assemble_down.1
  326.6 4.8 %collective-permute-done.51 = bf16[35,1024]{1,0:T(8,128)(2,1)S(1)} collective-permute-done((bf16[35,1024]{1,0:T(8,128)(2,1)S(1)}, bf16[35,1024]{1,0:T(8,128)(2,1)S(1)}, u32[]{:S(2)}, u32[]{:S(2)}) %collective-permute-start.51) | collective-permute-done | bytes 71712 | tf_op jit(solution)/shard_map/ppermute | solution.py:746
  (277 shorter events, 106.2 us)
Async XLA Ops:
  0.6 20.6 %collective-permute-start = (bf16[176,1024]{1,0:T(8,128)(2,1)}, bf16[176,1024]{1,0:T(8,128)(2,1)S(1)}, u32[]{:S(2)}, u32[]{:S(2)}) collective-permute-start(bf16[176,1024]{1,0:T(8,128)(2,1)} %tok_ref.1), channel_id=1, source_target_pairs={{0,2},{1,3},{2,4},{3,5},{4,6},{5,7},{6,0},{7,1},{8,10},{9,11},{10,... | collective-permute-start | bytes 1081352 | tf_op jit(solution)/shard_map/ppermute | solution.py:739
  2.8 18.8 %collective-permute-start.1 = (bf16[176,1024]{1,0:T(8,128)(2,1)}, bf16[176,1024]{1,0:T(8,128)(2,1)S(1)}, u32[]{:S(2)}, u32[]{:S(2)}) collective-permute-start(bf16[176,1024]{1,0:T(8,128)(2,1)} %tok_ref.1), channel_id=1, source_target_pairs={{0,6},{1,7},{2,0},{3,1},{4,2},{5,3},{6,4},{7,5},{8,14},{9,15},{10,... | collective-permute-start | bytes 1081352 | tf_op jit(solution)/shard_map/ppermute | solution.py:739
  4.1 17.7 %collective-permute-start.2 = (bf16[176,1024]{1,0:T(8,128)(2,1)}, bf16[176,1024]{1,0:T(8,128)(2,1)S(1)}, u32[]{:S(2)}, u32[]{:S(2)}) collective-permute-start(bf16[176,1024]{1,0:T(8,128)(2,1)} %tok_ref.1), channel_id=1, source_target_pairs={{0,4},{1,5},{2,6},{3,7},{4,0},{5,1},{6,2},{7,3},{8,12},{9,13},{10,... | collective-permute-start | bytes 1081352 | tf_op jit(solution)/shard_map/ppermute | solution.py:739
  11.2 30.1 %all-to-all-start = ((bf16[32,16,1024]{2,1,0:T(8,128)(2,1)}), bf16[32,16,1024]{2,1,0:T(8,128)(2,1)S(1)}, u32[]{:S(2)}, u32[]{:S(2)}) async-start(bf16[32,16,1024]{2,1,0:T(8,128)(2,1)} %bitcast.10), calls=%async_computation | async-start | bytes 2097152 | tf_op jit(solution)/shard_map/all_to_all | solution.py:762
  25.0 16.2 %collective-permute-start.7 = (bf16[128,1024]{1,0:T(8,128)(2,1)S(1)}, bf16[128,1024]{1,0:T(8,128)(2,1)}, u32[]{:S(2)}, u32[]{:S(2)}) collective-permute-start(bf16[128,1024]{1,0:T(8,128)(2,1)S(1)} %convert_element_type.63.refs_0_), channel_id=1, source_target_pairs={{0,2},{1,3},{2,4},{3,5},{4,6},{5,7},{6,0},{7,1},{8,10},{9,11},{10,... | collective-permute-start | bytes 786440 | tf_op jit(solution)/shard_map/ppermute | solution.py:739
  26.0 15.3 %collective-permute-start.8 = (bf16[128,1024]{1,0:T(8,128)(2,1)S(1)}, bf16[128,1024]{1,0:T(8,128)(2,1)}, u32[]{:S(2)}, u32[]{:S(2)}) collective-permute-start(bf16[128,1024]{1,0:T(8,128)(2,1)S(1)} %convert_element_type.63.refs_0_), channel_id=1, source_target_pairs={{0,6},{1,7},{2,0},{3,1},{4,2},{5,3},{6,4},{7,5},{8,14},{9,15},{10,... | collective-permute-start | bytes 786440 | tf_op jit(solution)/shard_map/ppermute | solution.py:739
  54.4 21.3 %collective-permute-start.14 = (bf16[416,1024]{1,0:T(8,128)(2,1)S(1)}, bf16[416,1024]{1,0:T(8,128)(2,1)S(1)}, u32[]{:S(2)}, u32[]{:S(2)}) collective-permute-start(bf16[416,1024]{1,0:T(8,128)(2,1)S(1)} %unpack.2.refs_1_.refs_0_), channel_id=1, source_target_pairs={{0,2},{1,3},{2,4},{3,5},{4,6},{5,7},{6,0},{7,1},{8,10},{9,11},{10,... | collective-permute-start | bytes 2555912 | tf_op jit(solution)/shard_map/ppermute | solution.py:739
  56.0 20.0 %collective-permute-start.15 = (bf16[416,1024]{1,0:T(8,128)(2,1)S(1)}, bf16[416,1024]{1,0:T(8,128)(2,1)}, u32[]{:S(2)}, u32[]{:S(2)}) collective-permute-start(bf16[416,1024]{1,0:T(8,128)(2,1)S(1)} %unpack.2.refs_1_.refs_0_), channel_id=1, source_target_pairs={{0,6},{1,7},{2,0},{3,1},{4,2},{5,3},{6,4},{7,5},{8,14},{9,15},{10,... | collective-permute-start | bytes 2555912 | tf_op jit(solution)/shard_map/ppermute | solution.py:739
  57.3 38.2 %collective-permute-start.16 = (bf16[416,1024]{1,0:T(8,128)(2,1)S(1)}, bf16[416,1024]{1,0:T(8,128)(2,1)}, u32[]{:S(2)}, u32[]{:S(2)}) collective-permute-start(bf16[416,1024]{1,0:T(8,128)(2,1)S(1)} %unpack.2.refs_1_.refs_0_), channel_id=1, source_target_pairs={{0,4},{1,5},{2,6},{3,7},{4,0},{5,1},{6,2},{7,3},{8,12},{9,13},{10,... | collective-permute-start | bytes 2555912 | tf_op jit(solution)/shard_map/ppermute | solution.py:739
  64.6 31.8 %all-to-all-start.2 = ((bf16[32,16,1024]{2,1,0:T(8,128)(2,1)}), bf16[32,16,1024]{2,1,0:T(8,128)(2,1)S(1)}, u32[]{:S(2)}, u32[]{:S(2)}) async-start(bf16[32,16,1024]{2,1,0:T(8,128)(2,1)} %bitcast.47), calls=%async_computation.2 | async-start | bytes 2097152 | tf_op jit(solution)/shard_map/all_to_all | solution.py:762
  74.1 26.0 %collective-permute-start.19 = (bf16[768,1024]{1,0:T(8,128)(2,1)}, bf16[768,1024]{1,0:T(8,128)(2,1)}, u32[]{:S(2)}, u32[]{:S(2)}) collective-permute-start(bf16[768,1024]{1,0:T(8,128)(2,1)} %get-tuple-element.261), channel_id=1, source_target_pairs={{0,1},{1,0},{2,3},{3,2},{4,5},{5,4},{6,7},{7,6},{8,9},{9,8},{10,11... | collective-permute-start | bytes 4718600 | tf_op jit(solution)/shard_map/ppermute | solution.py:742
  74.4 25.7 %collective-permute-start.20 = (bf16[384,1024]{1,0:T(8,128)(2,1)}, bf16[384,1024]{1,0:T(8,128)(2,1)}, u32[]{:S(2)}, u32[]{:S(2)}) collective-permute-start(bf16[384,1024]{1,0:T(8,128)(2,1)} %get-tuple-element.263), channel_id=1, source_target_pairs={{0,1},{1,0},{2,3},{3,2},{4,5},{5,4},{6,7},{7,6},{8,9},{9,8},{10,11... | collective-permute-start | bytes 2359304 | tf_op jit(solution)/shard_map/ppermute | solution.py:742
  97.3 21.2 %collective-permute-start.17 = (bf16[432,1024]{1,0:T(8,128)(2,1)S(1)}, bf16[432,1024]{1,0:T(8,128)(2,1)S(1)}, u32[]{:S(2)}, u32[]{:S(2)}) collective-permute-start(bf16[432,1024]{1,0:T(8,128)(2,1)S(1)} %unpack.3.refs_0_), channel_id=1, source_target_pairs={{0,2},{1,3},{2,4},{3,5},{4,6},{5,7},{6,0},{7,1},{8,10},{9,11},{10,... | collective-permute-start | bytes 2654216 | tf_op jit(solution)/shard_map/ppermute | solution.py:739
  97.9 20.6 %collective-permute-start.18 = (bf16[432,1024]{1,0:T(8,128)(2,1)S(1)}, bf16[432,1024]{1,0:T(8,128)(2,1)S(1)}, u32[]{:S(2)}, u32[]{:S(2)}) collective-permute-start(bf16[432,1024]{1,0:T(8,128)(2,1)S(1)} %unpack.3.refs_0_), channel_id=1, source_target_pairs={{0,6},{1,7},{2,0},{3,1},{4,2},{5,3},{6,4},{7,5},{8,14},{9,15},{10,... | collective-permute-start | bytes 2654216 | tf_op jit(solution)/shard_map/ppermute | solution.py:739
  118.6 17.4 %collective-permute-start.21 = (bf16[208,1024]{1,0:T(8,128)(2,1)S(1)}, bf16[208,1024]{1,0:T(8,128)(2,1)S(1)}, u32[]{:S(2)}, u32[]{:S(2)}) collective-permute-start(bf16[208,1024]{1,0:T(8,128)(2,1)S(1)} %slice.30), channel_id=1, source_target_pairs={{0,2},{1,3},{2,4},{3,5},{4,6},{5,7},{6,0},{7,1},{8,10},{9,11},{10,... | collective-permute-start | bytes 1277960 | tf_op jit(solution)/shard_map/ppermute | solution.py:739
  118.7 17.3 %collective-permute-start.22 = (bf16[224,1024]{1,0:T(8,128)(2,1)S(1)}, bf16[224,1024]{1,0:T(8,128)(2,1)S(1)}, u32[]{:S(2)}, u32[]{:S(2)}) collective-permute-start(bf16[224,1024]{1,0:T(8,128)(2,1)S(1)} %slice.31), channel_id=1, source_target_pairs={{0,6},{1,7},{2,0},{3,1},{4,2},{5,3},{6,4},{7,5},{8,14},{9,15},{10,... | collective-permute-start | bytes 1376264 | tf_op jit(solution)/shard_map/ppermute | solution.py:739
  177.9 21.1 %collective-permute-start.30 = (bf16[416,1024]{1,0:T(8,128)(2,1)S(1)}, bf16[416,1024]{1,0:T(8,128)(2,1)}, u32[]{:S(2)}, u32[]{:S(2)}) collective-permute-start(bf16[416,1024]{1,0:T(8,128)(2,1)S(1)} %get-tuple-element.346), channel_id=1, source_target_pairs={{0,6},{1,7},{2,0},{3,1},{4,2},{5,3},{6,4},{7,5},{8,14},{9,15},{10,... | collective-permute-start | bytes 2555912 | tf_op jit(solution)/shard_map/ppermute | solution.py:739
  179.6 20.0 %collective-permute-start.31 = (bf16[416,1024]{1,0:T(8,128)(2,1)S(1)}, bf16[416,1024]{1,0:T(8,128)(2,1)}, u32[]{:S(2)}, u32[]{:S(2)}) collective-permute-start(bf16[416,1024]{1,0:T(8,128)(2,1)S(1)} %get-tuple-element.347), channel_id=1, source_target_pairs={{0,2},{1,3},{2,4},{3,5},{4,6},{5,7},{6,0},{7,1},{8,10},{9,11},{10,... | collective-permute-start | bytes 2555912 | tf_op jit(solution)/shard_map/ppermute | solution.py:739
  181.7 27.2 %all-to-all-start.3 = ((bf16[32,16,1024]{2,1,0:T(8,128)(2,1)}), bf16[32,16,1024]{2,1,0:T(8,128)(2,1)}, u32[]{:S(2)}, u32[]{:S(2)}) async-start(bf16[32,16,1024]{2,1,0:T(8,128)(2,1)} %bitcast.20), calls=%async_computation.3 | async-start | bytes 2097152 | tf_op jit(solution)/shard_map/all_to_all | solution.py:762
  216.8 21.7 %collective-permute-start.34 = (bf16[4,128,1024]{2,1,0:T(8,128)(2,1)S(1)}, bf16[4,128,1024]{2,1,0:T(8,128)(2,1)S(1)}, u32[]{:S(2)}, u32[]{:S(2)}) collective-permute-start(bf16[4,128,1024]{2,1,0:T(8,128)(2,1)S(1)} %outer_sent.1), channel_id=1, source_target_pairs={{0,1},{1,0},{2,3},{3,2},{4,5},{5,4},{6,7},{7,6},{8,9},{9,8},{10,11... | collective-permute-start | bytes 3145736 | tf_op jit(solution)/shard_map/ppermute | solution.py:742
  220.3 20.1 %all-to-all-start.4 = ((bf16[8,176,128]{2,1,0:T(8,128)(2,1)}), bf16[8,176,128]{2,1,0:T(8,128)(2,1)}, u32[]{:S(2)}, u32[]{:S(2)}) async-start(bf16[8,176,128]{2,1,0:T(8,128)(2,1)} %get-tuple-element.374), calls=%async_computation.4 | async-start | bytes 720896 | tf_op jit(solution)/shard_map/all_to_all | solution.py:928
  240.4 30.5 %all-to-all-start.5 = ((bf16[32,16,1024]{2,1,0:T(8,128)(2,1)}), bf16[32,16,1024]{2,1,0:T(8,128)(2,1)S(1)}, u32[]{:S(2)}, u32[]{:S(2)}) async-start(bf16[32,16,1024]{2,1,0:T(8,128)(2,1)} %bitcast.23), calls=%async_computation.5 | async-start | bytes 2097152 | tf_op jit(solution)/shard_map/all_to_all | solution.py:762
  247.4 23.4 %collective-permute-start.35 = (bf16[128,1024]{1,0:T(8,128)(2,1)}, bf16[128,1024]{1,0:T(8,128)(2,1)S(1)}, u32[]{:S(2)}, u32[]{:S(2)}) collective-permute-start(bf16[128,1024]{1,0:T(8,128)(2,1)} %get-tuple-element.391), channel_id=1, source_target_pairs={{0,6},{1,7},{2,0},{3,1},{4,2},{5,3},{6,4},{7,5},{8,14},{9,15},{10,... | collective-permute-start | bytes 786440 | tf_op jit(solution)/shard_map/ppermute | solution.py:739
  247.5 23.4 %collective-permute-start.36 = (bf16[128,1024]{1,0:T(8,128)(2,1)}, bf16[128,1024]{1,0:T(8,128)(2,1)S(1)}, u32[]{:S(2)}, u32[]{:S(2)}) collective-permute-start(bf16[128,1024]{1,0:T(8,128)(2,1)} %get-tuple-element.392), channel_id=1, source_target_pairs={{0,2},{1,3},{2,4},{3,5},{4,6},{5,7},{6,0},{7,1},{8,10},{9,11},{10,... | collective-permute-start | bytes 786440 | tf_op jit(solution)/shard_map/ppermute | solution.py:739
  249.0 21.9 %collective-permute-start.37 = (bf16[128,1024]{1,0:T(8,128)(2,1)S(1)}, bf16[128,1024]{1,0:T(8,128)(2,1)S(1)}, u32[]{:S(2)}, u32[]{:S(2)}) collective-permute-start(bf16[128,1024]{1,0:T(8,128)(2,1)S(1)} %get-tuple-element.393), channel_id=1, source_target_pairs={{0,4},{1,5},{2,6},{3,7},{4,0},{5,1},{6,2},{7,3},{8,12},{9,13},{10,... | collective-permute-start | bytes 786440 | tf_op jit(solution)/shard_map/ppermute | solution.py:739
  274.2 23.6 %all-to-all-start.6 = ((bf16[16,32,1024]{2,1,0:T(8,128)(2,1)}), bf16[16,32,1024]{2,1,0:T(8,128)(2,1)}, u32[]{:S(2)}, u32[]{:S(2)}) async-start(bf16[16,32,1024]{2,1,0:T(8,128)(2,1)} %bitcast.34), calls=%async_computation.6 | async-start | bytes 2097152 | tf_op jit(solution)/shard_map/all_to_all | solution.py:960
  296.7 24.1 %collective-permute-start.52 = (bf16[1,352,1024]{2,1,0:T(8,128)(2,1)}, bf16[1,352,1024]{2,1,0:T(8,128)(2,1)}, u32[]{:S(2)}, u32[]{:S(2)}) collective-permute-start(bf16[1,352,1024]{2,1,0:T(8,128)(2,1)} %get-tuple-element.437), channel_id=1, source_target_pairs={{0,1},{1,0},{2,3},{3,2},{4,5},{5,4},{6,7},{7,6},{8,9},{9,8},{10,11... | collective-permute-start | bytes 2162696 | tf_op jit(solution)/shard_map/ppermute | solution.py:742
  297.8 17.5 %collective-permute-start.46 = (bf16[176,1024]{1,0:T(8,128)(2,1)}, bf16[176,1024]{1,0:T(8,128)(2,1)S(1)}, u32[]{:S(2)}, u32[]{:S(2)}) collective-permute-start(bf16[176,1024]{1,0:T(8,128)(2,1)} %copy-done.41), channel_id=1, source_target_pairs={{0,6},{1,7},{2,0},{3,1},{4,2},{5,3},{6,4},{7,5},{8,14},{9,15},{10,... | collective-permute-start | bytes 1081352 | tf_op jit(solution)/shard_map/ppermute | solution.py:739
  300.2 15.2 %collective-permute-start.47 = (bf16[176,1024]{1,0:T(8,128)(2,1)}, bf16[176,1024]{1,0:T(8,128)(2,1)}, u32[]{:S(2)}, u32[]{:S(2)}) collective-permute-start(bf16[176,1024]{1,0:T(8,128)(2,1)} %copy-done.40), channel_id=1, source_target_pairs={{0,2},{1,3},{2,4},{3,5},{4,6},{5,7},{6,0},{7,1},{8,10},{9,11},{10,... | collective-permute-start | bytes 1081352 | tf_op jit(solution)/shard_map/ppermute | solution.py:739
  300.2 16.6 %collective-permute-start.48 = (bf16[176,1024]{1,0:T(8,128)(2,1)}, bf16[176,1024]{1,0:T(8,128)(2,1)}, u32[]{:S(2)}, u32[]{:S(2)}) collective-permute-start(bf16[176,1024]{1,0:T(8,128)(2,1)} %copy-done.39), channel_id=1, source_target_pairs={{0,4},{1,5},{2,6},{3,7},{4,0},{5,1},{6,2},{7,3},{8,12},{9,13},{10,... | collective-permute-start | bytes 1081352 | tf_op jit(solution)/shard_map/ppermute | solution.py:739
  305.1 28.4 %all-to-all-start.7 = ((bf16[16,32,1024]{2,1,0:T(8,128)(2,1)}), bf16[16,32,1024]{2,1,0:T(8,128)(2,1)S(1)}, u32[]{:S(2)}, u32[]{:S(2)}) async-start(bf16[16,32,1024]{2,1,0:T(8,128)(2,1)} %copy-done.13), calls=%async_computation.7 | async-start | bytes 2097152 | tf_op jit(solution)/shard_map/all_to_all | solution.py:989
  316.8 14.7 %collective-permute-start.51 = (bf16[35,1024]{1,0:T(8,128)(2,1)S(1)}, bf16[35,1024]{1,0:T(8,128)(2,1)S(1)}, u32[]{:S(2)}, u32[]{:S(2)}) collective-permute-start(bf16[35,1024]{1,0:T(8,128)(2,1)S(1)} %add_add_fusion.1), channel_id=1, source_target_pairs={{0,96},{8,104},{16,112},{24,120},{32,64},{40,72},{48,80},{56,88},{... | collective-permute-start | bytes 215048 | tf_op jit(solution)/shard_map/ppermute | solution.py:746
  (94 other events, 775.3 us)
